TPU v7x, 128 devices: a whole 4x4x4 slice. The times are simulated.
128 devices in a mesh: tm: 16 (over x, z), space: 8 (over y, core).
Axes of the slice: x: 4, y: 4, z: 4, core: 2. Of those that a mesh axis runs over, the one named last changes fastest.
Arguments:
- source: float32 [32, 16, 256, 256], P('tm', 'space'), may hold values from -6 to 6
- start_field: float32 [16, 256, 256], P('space'), may hold values from -6 to 6
- last_guess: float32 [16, 256, 256], P('space'), may hold values from -6 to 6
- classes: int32 [16, 256, 256], P('space'), may hold values from 0 to 7
- conductivity: float32 [8], replicated, may hold values from 0.5 to 2
- alpha_num: int32 [1], replicated, may hold values from 4 to 16
Outputs:
- next_iterate: float32 [32, 16, 256, 256], P('tm', 'space')
Inputs may be any that keep to these rules, and one draw needn't show every extreme that they name: `classes`: each cell's class indexes the conductivity table. The circulant parameter is alpha_num / 32.
All inputs are finite; a program needn't handle non-finite values.
Results may differ from a plain program's by a relative error of at most 0.00014.
Values sent between devices are 32-bit elements; how exact they have to be, the bound alone decides.
A program may use at most 128 MiB of HBM per device.

v0:
```python
import functools

import jax
import jax.numpy as jnp
import numpy as np
from jax import lax
from jax.experimental import pallas as pl
from jax.experimental.pallas import tpu as pltpu
from jax.sharding import PartitionSpec as P

MESH = pl.DeviceIdType.MESH
F32 = jnp.float32
CHEB = 8
STEPS = 32
HALF_SPAN = 12.0
NTM, NSP = 16, 8
NDEV = NTM * NSP
LOWX, HIGHX, LOWY, HIGHY = 0, 1, 2, 3


def tables():
    lane = np.arange(128)
    slot, pair = lane // 8, lane % 8
    dft = np.zeros((2, 128, 2, 128))
    back = np.zeros((2, 128, 2, 128))
    same = (pair[:, None] == pair[None, :]).astype(np.float64)
    for half in range(2):
        n = 2 * slot + half
        angle = 2 * np.pi * ((n[:, None] * slot[None, :]) % STEPS) / STEPS
        sign = np.where(n % 2 == 0, 1.0, -1.0)[:, None]
        first = (slot == 0)[None, :]
        real = np.cos(angle)
        imag = np.where(first, sign, -np.sin(angle))
        weight = np.where(first, 1.0, 2.0) / STEPS
        dft[half, :, 0, :] = same * real
        dft[half, :, 1, :] = same * imag
        back[0, :, half, :] = (same * real * weight).T
        back[1, :, half, :] = (same * imag * weight).T
    trig = np.zeros((16, 128))
    for row in range(8):
        freq = np.where((slot == 0) & (row >= 4), 16, slot)
        angle = 2 * np.pi * freq / STEPS
        trig[row] = np.cos(angle)
        trig[8 + row] = np.where(slot == 0, 0.0, np.sin(angle))
    return (
        dft.reshape(256, 256).astype(np.float32),
        back.reshape(256, 256).astype(np.float32),
        trig.astype(np.float32),
    )


def cmul(a, b):
    return (a[0] * b[0] - a[1] * b[1], a[0] * b[1] + a[1] * b[0])


def cinv(a):
    denom = a[0] * a[0] + a[1] * a[1]
    return (a[0] / denom, -a[1] / denom)


def chebyshev_table(log_alpha, cos_f, sin_f):
    ratio = jnp.exp(log_alpha / STEPS)
    center = (1.0 - ratio * cos_f + HALF_SPAN, ratio * sin_f)
    sigma = (center[0] / HALF_SPAN, center[1] / HALF_SPAN)
    rho = [cinv(sigma)]
    for _ in range(CHEB):
        rho.append(cinv((2.0 * sigma[0] - rho[-1][0], 2.0 * sigma[1] - rho[-1][1])))
    inner = (jnp.ones_like(cos_f), jnp.zeros_like(cos_f))
    gains = [None] * (CHEB + 1)
    for j in range(CHEB, -1, -1):
        if j < CHEB:
            step = cmul(cmul(rho[j + 1], rho[j]), inner)
            inner = (1.0 + step[0], step[1])
        scale = cinv(center) if j == 0 else (rho[j][0] / 6.0, rho[j][1] / 6.0)
        gains[j] = cmul(scale, inner)
    level = (jnp.ones_like(cos_f), jnp.zeros_like(cos_f))
    terms = []
    for j in range(CHEB + 1):
        terms.append(cmul(gains[j], level))
        level = cmul(level, rho[j])
    zero = (jnp.zeros_like(cos_f), jnp.zeros_like(cos_f))
    terms += [zero, zero]
    out = []
    for j in range(CHEB + 1):
        own = terms[j] if j == 0 else (0.5 * terms[j][0], 0.5 * terms[j][1])
        out.append((own[0] - 0.5 * terms[j + 2][0], own[1] - 0.5 * terms[j + 2][1]))
    return out


def swap_groups(a):
    group = lax.broadcasted_iota(jnp.int32, a[0].shape, 1) // 32
    upper = group >= 2
    odd = group % 2 == 1
    c0 = jnp.where(upper, pltpu.roll(a[2], 64, 1), a[0])
    c2 = jnp.where(upper, a[2], pltpu.roll(a[0], 64, 1))
    c1 = jnp.where(upper, pltpu.roll(a[3], 64, 1), a[1])
    c3 = jnp.where(upper, a[3], pltpu.roll(a[1], 64, 1))
    return (
        jnp.where(odd, pltpu.roll(c1, 32, 1), c0),
        jnp.where(odd, c1, pltpu.roll(c0, 96, 1)),
        jnp.where(odd, pltpu.roll(c3, 32, 1), c2),
        jnp.where(odd, c3, pltpu.roll(c2, 96, 1)),
    )


def tile_of(tm, sp):
    cx, cz, cy, core = tm // 4, tm % 4, sp // 2, sp % 2
    zhi = cz // 2
    zlo = (cz + 1) // 2 % 2
    a = cx + zlo * (7 - 2 * cx)
    b = cy + zhi * (7 - 2 * cy)
    return 2 * a + core, b


def device_of(xi, yi):
    a, core = xi // 2, xi % 2
    zlo, zhi = a // 4, yi // 4
    cx = a + zlo * (7 - 2 * a)
    cy = yi + zhi * (7 - 2 * yi)
    cz = zlo + zhi * (3 - 2 * zlo)
    return cx * 4 + cz, cy * 2 + core


def dot(a, b):
    return jnp.dot(a, b, precision=lax.Precision.HIGHEST, preferred_element_type=F32)


def kernel(
    anum, cond, source, start, guess, classes, dft, back, trig, out,
    send1, recv1, send2, recv2, cls_send, cls_recv, kap, kys, kyr, wx, wym, wyp, wzi, wzm, wzp, wc,
    u, ys, yr, acc, beta, tsem, ksend, krecv, hsend, hrecv,
):
    tm = lax.axis_index("tm")
    sp = lax.axis_index("space")
    me = tm * NSP + sp
    xi, yi = tile_of(tm, sp)
    tile = xi * 8 + yi

    barrier = pltpu.get_barrier_semaphore()

    zrow = jnp.zeros((2, 2, 32, 128), F32)
    for slot in range(2):
        u[slot, 0] = zrow
        u[slot, 17] = zrow
        for side in range(2):
            yr[slot, side] = jnp.zeros((64, 128), F32)
    kap[0] = jnp.zeros((2, 32, 128), F32)
    kap[17] = jnp.zeros((2, 32, 128), F32)
    for side in range(2):
        kyr[side] = jnp.zeros((32, 128), F32)

    def greet(k, carry):
        t = (me + k) % NDEV
        pl.semaphore_signal(barrier, inc=1, device_id=(t // NSP, t % NSP), device_id_type=MESH)
        return carry

    lax.fori_loop(1, NDEV, greet, 0)

    log_alpha = jnp.log(jnp.full((8, 128), anum[0].astype(F32) / 32.0, F32))
    alpha_row = jnp.full((8, 128), anum[0].astype(F32) / 32.0, F32)
    first = jnp.where(tm == 0, 1.0, 0.0).astype(F32)
    n0 = (2 * tm).astype(F32)
    scales = [jnp.exp(log_alpha * (n0 + t) / STEPS) for t in range(2)]
    unscales = [jnp.exp(-log_alpha * (n0 + t) / STEPS) for t in range(2)]

    zhi = tm % 4 // 2
    half_lanes = pl.ds(pl.multiple_of(zhi * 128, 128), 128)
    for core in range(2):
        xc = (xi // 2) * 2 + core
        parts = [
            classes[z, pl.ds(pl.multiple_of(xc * 16 + xt * 8, 8), 8), half_lanes]
            for xt in range(2)
            for z in range(2)
        ]
        for j, value in enumerate(swap_groups(parts)):
            cls_send[core, j] = value

    def pack(x, carry):
        for xt in range(2):
            rows = pl.ds(pl.multiple_of(x * 16 + xt * 8, 8), 8)
            for h in range(2):
                lanes = slice(h * 128, h * 128 + 128)
                parts = []
                for t in range(2):
                    for z in range(2):
                        value = source[t, z, rows, lanes]
                        if t == 0:
                            value = value + (start[z, rows, lanes] - alpha_row * guess[z, rows, lanes]) * first
                        parts.append(value * scales[t])
                for j, value in enumerate(swap_groups(parts)):
                    at = pl.multiple_of((x * 8 + h * 4 + j) * 16 + xt * 8, 8)
                    send1[pl.ds(at, 8), :] = value
        return carry

    lax.fori_loop(0, 16, pack, 0)

    for j, (re, im) in enumerate(chebyshev_table(log_alpha, trig[0:8, :], trig[8:16, :])):
        beta[j, 0] = re
        beta[j, 1] = im

    pl.semaphore_wait(barrier, NDEV - 1)

    def cls_go(k, carry):
        other = (sp + k) % NSP
        ocy, ocore = other // 2, other % 2
        j = ocy + zhi * (3 - 2 * ocy)
        pltpu.make_async_remote_copy(
            src_ref=cls_send.at[ocore, j],
            dst_ref=cls_recv.at[pl.ds(pl.multiple_of(sp * 8, 8), 8)],
            send_sem=tsem.at[4],
            recv_sem=tsem.at[5],
            device_id=(tm, other),
            device_id_type=MESH,
        ).start()
        return carry

    lax.fori_loop(1, NSP, cls_go, 0)

    def rows16(index):
        return pl.ds(pl.multiple_of(index * 16, 16), 16)

    def t1_go(k, carry):
        kk = (k * 37) % NDEV
        t0 = (tm // 4 + kk // 32) % 4 * 4 + (tm + kk // 8) % 4
        t1 = (sp // 2 + kk // 2) % 4 * 2 + (sp + kk) % 2
        ox, oy = tile_of(t0, t1)
        pltpu.make_async_remote_copy(
            src_ref=send1.at[rows16(ox * 8 + oy)],
            dst_ref=recv1.at[rows16(me)],
            send_sem=tsem.at[0],
            recv_sem=tsem.at[1],
            device_id=(t0, t1),
            device_id_type=MESH,
        ).start()
        return carry

    lax.fori_loop(1, NDEV, t1_go, 0)
    recv1[rows16(me), :] = send1[rows16(tile), :]
    mycy, mycore = sp // 2, sp % 2
    cls_recv[pl.ds(pl.multiple_of(sp * 8, 8), 8), :] = cls_send[mycore, mycy + zhi * (3 - 2 * mycy)]

    some = cls_recv.at[pl.ds(0, 56)]
    pltpu.make_async_copy(some, some, tsem.at[5]).wait()

    def conductivities(xx, carry):
        codes = cls_recv[pl.ds(xx, 8, stride=8), :]
        value = jnp.zeros((8, 128), F32)
        for level in range(8):
            value = jnp.where(codes == level, cond[level], value)
        full = jnp.concatenate([value] * 16, axis=0).T
        for xt in range(2):
            block = full[xt * 64 : xt * 64 + 64].reshape(2, 32, 128)
            kap[1 + xt * 8 + xx] = block
            for z in range(2):
                row = pl.ds((xt * 8 + xx) * 2 + z, 1)
                kys[0, row, :] = block[z, 0:1]
                kys[1, row, :] = block[z, 31:32]
        return carry

    lax.fori_loop(0, 8, conductivities, 0)

    has = [xi > 0, xi < 15, yi > 0, yi < 7]
    near = [
        device_of(jnp.maximum(xi - 1, 0), yi),
        device_of(jnp.minimum(xi + 1, 15), yi),
        device_of(xi, jnp.maximum(yi - 1, 0)),
        device_of(xi, jnp.minimum(yi + 1, 7)),
    ]

    def kap_copy(side):
        src, dst = [
            (kap.at[1], kap.at[17]),
            (kap.at[16], kap.at[0]),
            (kys.at[0], kyr.at[1]),
            (kys.at[1], kyr.at[0]),
        ][side]
        return pltpu.make_async_remote_copy(
            src_ref=src, dst_ref=dst, send_sem=ksend.at[side], recv_sem=krecv.at[side ^ 1],
            device_id=near[side], device_id_type=MESH,
        )

    def kap_wait(side):
        dst = [kap.at[0], kap.at[17], kyr.at[0], kyr.at[1]][side]
        pltpu.make_async_copy(dst, dst, krecv.at[side]).wait()

    def u_copy(slot, side):
        src, dst = [
            (u.at[slot, 1], u.at[slot, 17]),
            (u.at[slot, 16], u.at[slot, 0]),
            (ys.at[slot, 0], yr.at[slot, 1]),
            (ys.at[slot, 1], yr.at[slot, 0]),
        ][side]
        return pltpu.make_async_remote_copy(
            src_ref=src, dst_ref=dst, send_sem=hsend.at[slot, side], recv_sem=hrecv.at[slot, side ^ 1],
            device_id=near[side], device_id_type=MESH,
        )

    def u_wait(slot, side):
        dst = [u.at[slot, 0], u.at[slot, 17], yr.at[slot, 0], yr.at[slot, 1]][side]
        pltpu.make_async_copy(dst, dst, hrecv.at[slot, side]).wait()

    for side in range(4):

        @pl.when(has[side])
        def _(side=side):
            kap_copy(side).start()

    for side in range(4):

        @pl.when(has[side])
        def _(side=side):
            kap_wait(side)

    row_at = lax.broadcasted_iota(jnp.int32, (32, 128), 0)
    pair_at = lax.broadcasted_iota(jnp.int32, (32, 128), 1) % 8

    def weights(x, carry):
        total = [None, None]
        k = [kap[x + 1, z] for z in range(2)]
        for z in range(2):
            row = pl.ds(x * 2 + z, 1)
            low = (k[z] + kap[x, z]) * (1.0 / 12.0)
            high = (k[z] + kap[x + 2, z]) * (1.0 / 12.0)
            wx[x, z] = low

            @pl.when(x == 15)
            def _(z=z, high=high):
                wx[16, z] = high

            before = jnp.where(row_at == 0, kyr[0, row, :], pltpu.roll(k[z], 1, 0))
            after = jnp.where(row_at == 31, kyr[1, row, :], pltpu.roll(k[z], 31, 0))
            before = (k[z] + before) * (1.0 / 12.0)
            after = (k[z] + after) * (1.0 / 12.0)
            wym[x, z] = before
            wyp[x, z] = after
            total[z] = (low + high) + (before + after)
        inside = (k[0] + k[1]) * (1.0 / 12.0)
        below = (k[0] + jnp.where(pair_at == 0, 0.0, pltpu.roll(k[1], 1, 1))) * (1.0 / 12.0)
        above = (k[1] + jnp.where(pair_at == 7, 0.0, pltpu.roll(k[0], 127, 1))) * (1.0 / 12.0)
        wzi[x] = inside
        wzm[x] = jnp.where(pair_at == 0, 0.0, below)
        wzp[x] = jnp.where(pair_at == 7, 0.0, above)
        wc[x, 0] = 2.0 - (total[0] + (inside + below))
        wc[x, 1] = 2.0 - (total[1] + (inside + above))
        return carry

    lax.fori_loop(0, 16, weights, 0)

    most = recv1.at[pl.ds(0, (NDEV - 1) * 16)]
    pltpu.make_async_copy(most, most, tsem.at[1]).wait()

    def put_edges(slot, x, p, z, value):
        row = pl.ds(x * 4 + p * 2 + z, 1)
        ys[slot, 0, row, :] = value[0:1]
        ys[slot, 1, row, :] = value[31:32]

    def forward(x, carry):
        cells = recv1[pl.ds(x, 128, stride=16), :].T
        spectrum = dot(jnp.concatenate([cells[:64], cells[64:]], axis=1), dft[...])
        for p in range(2):
            for z in range(2):
                value = spectrum[z * 32 : z * 32 + 32, p * 128 : p * 128 + 128]
                u[0, x + 1, p, z] = value
                u[1, x + 1, p, z] = jnp.zeros((32, 128), F32)
                put_edges(0, x, p, z, value)
        return carry

    lax.fori_loop(0, 16, forward, 0)

    for j in range(CHEB):
        now, new = j % 2, (j + 1) % 2
        last = j == CHEB - 1
        for side in range(4):

            @pl.when(has[side])
            def _(side=side, now=now):
                u_copy(now, side).start()

        for side in range(4):

            @pl.when(has[side])
            def _(side=side, now=now):
                u_wait(now, side)
                u_copy(now, side).wait_send()

        def sweep(x, carry, j=j, now=now, new=new, last=last):
            got = []
            for p in range(2):
                mid = [u[now, x + 1, p, z] for z in range(2)]
                for z in range(2):
                    row = pl.ds(x * 4 + p * 2 + z, 1)
                    before = jnp.where(row_at == 0, yr[now, 0, row, :], pltpu.roll(mid[z], 1, 0))
                    after = jnp.where(row_at == 31, yr[now, 1, row, :], pltpu.roll(mid[z], 31, 0))
                    total = wc[x, z] * mid[z]
                    total = total + (wx[x, z] * u[now, x, p, z] + wx[x + 1, z] * u[now, x + 2, p, z])
                    total = total + (wym[x, z] * before + wyp[x, z] * after)
                    if z == 0:
                        total = total + (wzi[x] * mid[1] + wzm[x] * pltpu.roll(mid[1], 1, 1))
                    else:
                        total = total + (wzi[x] * mid[0] + wzp[x] * pltpu.roll(mid[0], 127, 1))
                    prev = u[new, x + 1, p, z]
                    value = total - prev
                    if not last:
                        u[new, x + 1, p, z] = value
                        put_edges(new, x, p, z, value)
                    got.append((prev, mid[z], value))
            if j % 3 == 1:
                for z in range(2):
                    real, imag = None, None
                    for i in range(3):
                        a, b = got[z][i], got[2 + z][i]
                        br0, br1 = beta[j - 1 + i, 0, 0:1, :], beta[j - 1 + i, 0, 4:5, :]
                        bi = beta[j - 1 + i, 1, 0:1, :]
                        re = br0 * a - bi * b
                        im = br1 * b + bi * a
                        real = re if real is None else real + re
                        imag = im if imag is None else imag + im
                    if j > 1:
                        real = real + acc[x, 0, z]
                        imag = imag + acc[x, 1, z]
                    acc[x, 0, z] = real
                    acc[x, 1, z] = imag
            return carry

        lax.fori_loop(0, 16, sweep, 0)

    def inverse(x, carry):
        both = jnp.concatenate([acc[x, 0].reshape(64, 128), acc[x, 1].reshape(64, 128)], axis=1)
        times = dot(both, back[...])
        cells = jnp.concatenate([times[:, :128], times[:, 128:]], axis=0)
        send2[pl.ds(x, 128, stride=16), :] = cells.T
        return carry

    lax.fori_loop(0, 16, inverse, 0)

    def t2_go(k, carry):
        kk = (k * 37) % NDEV
        t0 = (tm // 4 + kk // 32) % 4 * 4 + (tm + kk // 8) % 4
        t1 = (sp // 2 + kk // 2) % 4 * 2 + (sp + kk) % 2
        pltpu.make_async_remote_copy(
            src_ref=send2.at[rows16(t0 * NSP + t1)],
            dst_ref=recv2.at[rows16(tile)],
            send_sem=tsem.at[2],
            recv_sem=tsem.at[3],
            device_id=(t0, t1),
            device_id_type=MESH,
        ).start()
        return carry

    lax.fori_loop(1, NDEV, t2_go, 0)
    recv2[rows16(tile), :] = send2[rows16(me), :]
    most2 = recv2.at[pl.ds(0, (NDEV - 1) * 16)]
    pltpu.make_async_copy(most2, most2, tsem.at[3]).wait()

    def unpack(x, carry):
        for xt in range(2):
            rows = pl.ds(pl.multiple_of(x * 16 + xt * 8, 8), 8)
            for h in range(2):
                parts = [
                    recv2[pl.ds(pl.multiple_of((x * 8 + h * 4 + j) * 16 + xt * 8, 8), 8), :]
                    for j in range(4)
                ]
                for i, value in enumerate(swap_groups(parts)):
                    out[i // 2, i % 2, rows, h * 128 : h * 128 + 128] = value * unscales[i // 2]
        return carry

    lax.fori_loop(0, 16, unpack, 0)

    pltpu.make_async_copy(most, most, tsem.at[0]).wait()
    pltpu.make_async_copy(most2, most2, tsem.at[2]).wait()
    pltpu.make_async_copy(some, some, tsem.at[4]).wait()
    for side in range(4):

        @pl.when(has[side])
        def _(side=side):
            kap_copy(side).wait_send()


def body(source, start_field, last_guess, classes, conductivity, alpha_num):
    dft, back, trig = (jnp.asarray(t) for t in tables())
    smem = pl.BlockSpec(memory_space=pltpu.SMEM)
    vmem = pl.BlockSpec(memory_space=pltpu.VMEM)
    V = pltpu.VMEM
    return pl.pallas_call(
        kernel,
        out_shape=jax.ShapeDtypeStruct((2, 2, 256, 256), F32),
        in_specs=[smem, smem] + [vmem] * 7,
        out_specs=vmem,
        scratch_shapes=[
            V((2048, 128), F32), V((2048, 128), F32), V((2048, 128), F32), V((2048, 128), F32),
            V((2, 4, 8, 128), jnp.int32), V((64, 128), jnp.int32),
            V((18, 2, 32, 128), F32), V((2, 32, 128), F32), V((2, 32, 128), F32),
            V((17, 2, 32, 128), F32), V((16, 2, 32, 128), F32), V((16, 2, 32, 128), F32),
            V((16, 32, 128), F32), V((16, 32, 128), F32), V((16, 32, 128), F32), V((16, 2, 32, 128), F32),
            V((2, 18, 2, 2, 32, 128), F32), V((2, 2, 64, 128), F32), V((2, 2, 64, 128), F32),
            V((16, 2, 2, 32, 128), F32), V((CHEB + 1, 2, 8, 128), F32),
            pltpu.SemaphoreType.DMA((6,)),
            pltpu.SemaphoreType.DMA((4,)), pltpu.SemaphoreType.DMA((4,)),
            pltpu.SemaphoreType.DMA((2, 4)), pltpu.SemaphoreType.DMA((2, 4)),
        ],
        compiler_params=pltpu.CompilerParams(
            collective_id=1, has_side_effects=True, vmem_limit_bytes=48 * 2**20
        ),
    )(alpha_num, conductivity, source, start_field, last_guess, classes, dft, back, trig)


def solution(mesh):
    placed = (
        P("tm", "space", None, None),
        P("space", None, None),
        P("space", None, None),
        P("space", None, None),
        P(),
        P(),
    )
    return jax.shard_map(
        body, mesh=mesh, in_specs=placed, out_specs=P("tm", "space", None, None), check_vma=False
    )
```

profile of v0, /device:TPU:1, one launch (start us, length us, event | category | flops | bytes accessed | tf_op | source)
XLA Modules:
  0.0 104.4 jit_solution(12621673025152512439)
XLA Ops:
  0.0 0.0 copy-start.7
  0.7 0.0 copy-done.7
  0.7 0.0 copy-start
  0.7 1.2 %copy-done = f32[2,2,256,256]{3,2,1,0:T(8,128)S(1)} copy-done((f32[2,2,256,256]{3,2,1,0:T(8,128)S(1)}, f32[2,2,256,256]{3,2,1,0:T(8,128)}, u32[]{:S(2)}) %copy-start) | copy-done | bytes 1048600
  1.9 0.0 copy-start.1
  1.9 1.0 copy-done.1
  2.9 0.0 copy-start.2
  2.9 1.0 copy-done.2
  4.0 0.0 copy-start.3
  4.0 1.0 copy-done.3
  5.0 0.0 copy-start.4
  5.0 0.9 copy-done.4
  6.0 0.0 copy-start.5
  6.0 0.9 copy-done.5
  6.9 0.0 copy-start.6
  6.9 0.7 copy-done.6
  7.6 95.8 %shard_map.91 = f32[2,2,256,256]{3,2,1,0:T(8,128)S(1)} custom-call(s32[1]{0:T(128)S(6)} %copy.11.anum, f32[8]{0:T(128)S(1)} %copy-done.7, f32[2,2,256,256]{3,2,1,0:T(8,128)S(1)} %copy-done, f32[2,256,256]{2,1,0:T(8,128)S(1)} %copy-done.1, f32[2,256,256]{2,1,0:T(8,128)S(1)} %copy-done.2, s32[2,256,256]{2,1,0:T(8,128)S(1)} %copy-done.3, ...), custom_call_target="tpu_custom_call" | custom-call | tf_op jit(solution)/shard_map/pallas_call | solution.py:484
  103.5 1.0 copy.12
Async XLA Ops:
  0.0 0.7 copy-start.7
  0.7 1.2 %copy-start = (f32[2,2,256,256]{3,2,1,0:T(8,128)S(1)}, f32[2,2,256,256]{3,2,1,0:T(8,128)}, u32[]{:S(2)}) copy-start(f32[2,2,256,256]{3,2,1,0:T(8,128)} %source.1) | copy-start | bytes 3145732
  1.9 1.0 copy-start.1
  2.9 1.0 copy-start.2
  4.0 1.0 copy-start.3
  5.0 0.9 copy-start.4
  6.0 0.9 copy-start.5
  6.9 0.7 copy-start.6
where the time goes:
time: 105 us; the launch traced here: 104 us
  Pallas kernels  95.8 us (91%)
  local copies, waits for them, and re-layouts  7.91 us (8%)
    pallas_call x1, Pallas kernels, body(): pl.pallas_call(kernel, out_shape=jax.ShapeDtypeStruct((2, 2, 256, 256), F...  95.8 us
    unnamed x17, local copies, waits for them, and re-layouts  7.91 us

commit v1 on v0

v1 whole, which is shorter than its diff:
```python
import functools

import jax
import jax.numpy as jnp
import numpy as np
from jax import lax
from jax.experimental import pallas as pl
from jax.experimental.pallas import tpu as pltpu
from jax.sharding import PartitionSpec as P

MESH = pl.DeviceIdType.MESH
F32 = jnp.float32
CHEB = 8
STEPS = 32
HALF_SPAN = 12.0
NTM, NSP = 16, 8
NDEV = NTM * NSP
DEPTH = 4
BLOCK = 4
UNROLL = 2
SIDES = [(dx, dy) for dx in (-1, 0, 1) for dy in (-1, 0, 1) if (dx, dy) != (0, 0)]


def tables():
    lane = np.arange(128)
    slot, pair = lane // 8, lane % 8
    dft = np.zeros((2, 128, 2, 128))
    back = np.zeros((2, 128, 2, 128))
    same = (pair[:, None] == pair[None, :]).astype(np.float64)
    for half in range(2):
        n = 2 * slot + half
        angle = 2 * np.pi * ((n[:, None] * slot[None, :]) % STEPS) / STEPS
        sign = np.where(n % 2 == 0, 1.0, -1.0)[:, None]
        first = (slot == 0)[None, :]
        real = np.cos(angle)
        imag = np.where(first, sign, -np.sin(angle))
        weight = np.where(first, 1.0, 2.0) / STEPS
        dft[half, :, 0, :] = same * real
        dft[half, :, 1, :] = same * imag
        back[0, :, half, :] = (same * real * weight).T
        back[1, :, half, :] = (same * imag * weight).T
    trig = np.zeros((16, 128))
    for row in range(8):
        freq = np.where((slot == 0) & (row >= 4), 16, slot)
        angle = 2 * np.pi * freq / STEPS
        trig[row] = np.cos(angle)
        trig[8 + row] = np.where(slot == 0, 0.0, np.sin(angle))
    return (
        dft.reshape(256, 256).astype(np.float32),
        back.reshape(256, 256).astype(np.float32),
        trig.astype(np.float32),
    )


def cmul(a, b):
    return (a[0] * b[0] - a[1] * b[1], a[0] * b[1] + a[1] * b[0])


def cinv(a):
    denom = a[0] * a[0] + a[1] * a[1]
    return (a[0] / denom, -a[1] / denom)


def chebyshev_table(log_alpha, cos_f, sin_f):
    ratio = jnp.exp(log_alpha / STEPS)
    center = (1.0 - ratio * cos_f + HALF_SPAN, ratio * sin_f)
    sigma = (center[0] / HALF_SPAN, center[1] / HALF_SPAN)
    rho = [cinv(sigma)]
    for _ in range(CHEB):
        rho.append(cinv((2.0 * sigma[0] - rho[-1][0], 2.0 * sigma[1] - rho[-1][1])))
    inner = (jnp.ones_like(cos_f), jnp.zeros_like(cos_f))
    gains = [None] * (CHEB + 1)
    for j in range(CHEB, -1, -1):
        if j < CHEB:
            step = cmul(cmul(rho[j + 1], rho[j]), inner)
            inner = (1.0 + step[0], step[1])
        scale = cinv(center) if j == 0 else (rho[j][0] / 6.0, rho[j][1] / 6.0)
        gains[j] = cmul(scale, inner)
    level = (jnp.ones_like(cos_f), jnp.zeros_like(cos_f))
    terms = []
    for j in range(CHEB + 1):
        terms.append(cmul(gains[j], level))
        level = cmul(level, rho[j])
    zero = (jnp.zeros_like(cos_f), jnp.zeros_like(cos_f))
    terms += [zero, zero]
    out = []
    for j in range(CHEB + 1):
        own = terms[j] if j == 0 else (0.5 * terms[j][0], 0.5 * terms[j][1])
        out.append((own[0] - 0.5 * terms[j + 2][0], own[1] - 0.5 * terms[j + 2][1]))
    for m in range(BLOCK, 0, -1):
        for j in range(BLOCK + m - 2, BLOCK - m - 1, -2):
            out[j] = (out[j][0] - out[BLOCK + m][0], out[j][1] - out[BLOCK + m][1])
    return out


def swap_groups(a):
    group = lax.broadcasted_iota(jnp.int32, a[0].shape, 1) // 32
    upper = group >= 2
    odd = group % 2 == 1
    c0 = jnp.where(upper, pltpu.roll(a[2], 64, 1), a[0])
    c2 = jnp.where(upper, a[2], pltpu.roll(a[0], 64, 1))
    c1 = jnp.where(upper, pltpu.roll(a[3], 64, 1), a[1])
    c3 = jnp.where(upper, a[3], pltpu.roll(a[1], 64, 1))
    return (
        jnp.where(odd, pltpu.roll(c1, 32, 1), c0),
        jnp.where(odd, c1, pltpu.roll(c0, 96, 1)),
        jnp.where(odd, pltpu.roll(c3, 32, 1), c2),
        jnp.where(odd, c3, pltpu.roll(c2, 96, 1)),
    )


def tile_of(tm, sp):
    cx, cz, cy, core = tm // 4, tm % 4, sp // 2, sp % 2
    zhi = cz // 2
    zlo = (cz + 1) // 2 % 2
    a = cx + zlo * (7 - 2 * cx)
    b = cy + zhi * (7 - 2 * cy)
    return 2 * a + core, b


def device_of(xi, yi):
    a, core = xi // 2, xi % 2
    zlo, zhi = a // 4, yi // 4
    cx = a + zlo * (7 - 2 * a)
    cy = yi + zhi * (7 - 2 * yi)
    cz = zlo + zhi * (3 - 2 * zlo)
    return cx * 4 + cz, cy * 2 + core


def two_terms(a):
    head = a.astype(jnp.bfloat16)
    return head, (a - head.astype(F32)).astype(jnp.bfloat16)


def dot(a, head, rest):
    a_head, a_rest = two_terms(a)
    small = jnp.dot(a_rest, head, preferred_element_type=F32) + jnp.dot(a_head, rest, preferred_element_type=F32)
    return jnp.dot(a_head, head, preferred_element_type=F32) + small


def kernel(
    anum, cond, source_in, start_in, guess_in, classes_in, dft_in, back_in, trig_in, out,
    source, start, guess, classes, dft, back, dft0, dft1, back0, back1, trig, insem, send1, recv1, send2, recv2, cls_send, cls_recv, kap, wxm, wxp, wym, wyp, wzi, wzm, wzp, wc,
    u0, u1, u2, u3, acc, beta, tsem, ksend, krecv, hsend, hrecv, outsem,
):
    tm = lax.axis_index("tm")
    sp = lax.axis_index("space")
    me = tm * NSP + sp
    xi, yi = tile_of(tm, sp)
    tile = xi * 8 + yi

    zhi = tm % 4 // 2
    half_lanes = pl.ds(pl.multiple_of(zhi * 128, 128), 128)
    pair_rows = pl.ds(pl.multiple_of(xi // 2 * 32, 32), 32)
    pairs = [
        (source_in, source),
        (classes_in.at[:, pair_rows, half_lanes], classes),
        (trig_in, trig),
        (dft_in, dft),
        (back_in, back),
    ]
    loads = [pltpu.make_async_copy(a, b, insem.at[i]) for i, (a, b) in enumerate(pairs)]
    firsts = [
        pltpu.make_async_copy(start_in, start, insem.at[5]),
        pltpu.make_async_copy(guess_in, guess, insem.at[6]),
    ]
    for copy in loads:
        copy.start()

    @pl.when(tm == 0)
    def _():
        for copy in firsts:
            copy.start()

    barrier = pltpu.get_barrier_semaphore()

    def clear(x, carry):
        kap[x] = jnp.zeros((2, 40, 128), F32)
        for p in range(2):
            u0[p, x] = jnp.zeros((2, 40, 128), F32)
            u3[p, x] = jnp.zeros((2, 40, 128), F32)
        return carry

    lax.fori_loop(0, 24, clear, 0)

    def greet(k, carry):
        t = (me + k) % NDEV
        pl.semaphore_signal(barrier, inc=1, device_id=(t // NSP, t % NSP), device_id_type=MESH)
        return carry

    lax.fori_loop(1, NDEV, greet, 0)

    log_alpha = jnp.log(jnp.full((8, 128), anum[0].astype(F32) / 32.0, F32))
    alpha = anum[0].astype(F32) / 32.0
    n0 = (2 * tm).astype(F32)
    scales = [jnp.exp(log_alpha * (n0 + t) / STEPS) for t in range(2)]
    unscales = [jnp.exp(-log_alpha * (n0 + t) / STEPS) for t in range(2)]

    loads[1].wait()
    for core in range(2):
        parts = [
            classes[z, core * 16 + xt * 8 : core * 16 + xt * 8 + 8, :]
            for xt in range(2)
            for z in range(2)
        ]
        for j, value in enumerate(swap_groups(parts)):
            cls_send[core, j] = value

    loads[0].wait()

    @pl.when(tm == 0)
    def _():
        for copy in firsts:
            copy.wait()

        def correct(x, carry):
            rows = pl.ds(pl.multiple_of(x * 16, 16), 16)
            for z in range(2):
                source[0, z, rows, :] = source[0, z, rows, :] + (start[z, rows, :] - alpha * guess[z, rows, :])
            return carry

        lax.fori_loop(0, 16, correct, 0)

    def pack(x, carry):
        for xt in range(2):
            rows = pl.ds(pl.multiple_of(x * 16 + xt * 8, 8), 8)
            for h in range(2):
                lanes = slice(h * 128, h * 128 + 128)
                parts = []
                for t in range(2):
                    for z in range(2):
                        value = source[t, z, rows, lanes]
                        parts.append(value * scales[t])
                for j, value in enumerate(swap_groups(parts)):
                    at = pl.multiple_of((x * 8 + h * 4 + j) * 16 + xt * 8, 8)
                    send1[pl.ds(at, 8), :] = value
        return carry

    lax.fori_loop(0, 16, pack, 0)

    for copy in loads[2:]:
        copy.wait()
    dft0[...], dft1[...] = two_terms(dft[...])
    back0[...], back1[...] = two_terms(back[...])
    for j, (re, im) in enumerate(chebyshev_table(log_alpha, trig[0:8, :], trig[8:16, :])):
        beta[j, 0:1, :] = re[0:1]
        beta[j, 1:2, :] = im[0:1]
        beta[j, 2:3, :] = -im[0:1]
        beta[j, 3:4, :] = re[4:5]

    pl.semaphore_wait(barrier, NDEV - 1)

    def cls_go(k, carry):
        other = (sp + k) % NSP
        ocy, ocore = other // 2, other % 2
        j = ocy + zhi * (3 - 2 * ocy)
        pltpu.make_async_remote_copy(
            src_ref=cls_send.at[ocore, j],
            dst_ref=cls_recv.at[pl.ds(pl.multiple_of(sp * 8, 8), 8)],
            send_sem=tsem.at[4],
            recv_sem=tsem.at[5],
            device_id=(tm, other),
            device_id_type=MESH,
        ).start()
        return carry

    lax.fori_loop(1, NSP, cls_go, 0)

    def rows16(index):
        return pl.ds(pl.multiple_of(index * 16, 16), 16)

    def t1_go(k, carry):
        kk = (k * 37) % NDEV
        t0 = (tm // 4 + kk // 32) % 4 * 4 + (tm + kk // 8) % 4
        t1 = (sp // 2 + kk // 2) % 4 * 2 + (sp + kk) % 2
        ox, oy = tile_of(t0, t1)
        pltpu.make_async_remote_copy(
            src_ref=send1.at[rows16(ox * 8 + oy)],
            dst_ref=recv1.at[rows16(me)],
            send_sem=tsem.at[0],
            recv_sem=tsem.at[1],
            device_id=(t0, t1),
            device_id_type=MESH,
        ).start()
        return carry

    lax.fori_loop(1, NDEV, t1_go, 0)
    recv1[rows16(me), :] = send1[rows16(tile), :]
    mycy, mycore = sp // 2, sp % 2
    cls_recv[pl.ds(pl.multiple_of(sp * 8, 8), 8), :] = cls_send[mycore, mycy + zhi * (3 - 2 * mycy)]

    some = cls_recv.at[pl.ds(0, 56)]
    pltpu.make_async_copy(some, some, tsem.at[5]).wait()

    def conductivities(xx, carry):
        codes = cls_recv[pl.ds(xx, 8, stride=8), :]
        value = jnp.zeros((8, 128), F32)
        for level in range(8):
            value = jnp.where(codes == level, cond[level], value)
        full = jnp.concatenate([value] * 16, axis=0).T
        for xt in range(2):
            kap[DEPTH + xt * 8 + xx, :, 0:32, :] = full[xt * 64 : xt * 64 + 64].reshape(2, 32, 128)
        return carry

    lax.fori_loop(0, 8, conductivities, 0)

    low_x, high_x, low_y, high_y = xi > 0, xi < 15, yi > 0, yi < 7
    beside = {-1: low_x, 1: high_x}, {-1: low_y, 1: high_y}

    def here(dx, dy):
        if dx and dy:
            return jnp.logical_and(beside[0][dx], beside[1][dy])
        return beside[0][dx] if dx else beside[1][dy]

    def span(d, low, middle, high):
        return {-1: low, 0: middle, 1: high}[d]

    def halo(dx, dy):
        return (
            span(dx, pl.ds(0, DEPTH), pl.ds(DEPTH, 16), pl.ds(DEPTH + 16, DEPTH)),
            span(dy, pl.ds(36, 4), pl.ds(0, 32), pl.ds(32, 4)),
        )

    def edge(dx, dy):
        return (
            span(dx, pl.ds(DEPTH, DEPTH), pl.ds(DEPTH, 16), pl.ds(16, DEPTH)),
            span(dy, pl.ds(0, 4), pl.ds(0, 32), pl.ds(28, 4)),
        )

    def exchange(ref, send, recv, act):
        for i, (dx, dy) in enumerate(SIDES):

            @pl.when(here(dx, dy))
            def _(i=i, dx=dx, dy=dy):
                xs, ys = edge(dx, dy)
                xd, yd = halo(-dx, -dy)
                back_at = SIDES.index((-dx, -dy))
                copy = pltpu.make_async_remote_copy(
                    src_ref=ref.at[xs, :, ys, :],
                    dst_ref=ref.at[xd, :, yd, :],
                    send_sem=send.at[i],
                    recv_sem=recv.at[back_at],
                    device_id=device_of(
                        jnp.clip(xi + dx, 0, 15) if dx else xi, jnp.clip(yi + dy, 0, 7) if dy else yi
                    ),
                    device_id_type=MESH,
                )
                if act == "start":
                    copy.start()
                else:
                    copy.wait_send()
                    xh, yh = halo(dx, dy)
                    got = ref.at[xh, :, yh, :]
                    pltpu.make_async_copy(got, got, recv.at[i]).wait()

    exchange(kap, ksend, krecv, "start")
    exchange(kap, ksend, krecv, "wait")

    row_at = lax.broadcasted_iota(jnp.int32, (40, 128), 0)
    pair_at = lax.broadcasted_iota(jnp.int32, (40, 128), 1) % 8
    one = jnp.ones((40, 128), F32)
    inside_low = jnp.where(low_y, 1.0, 0.0).astype(F32)
    inside_high = jnp.where(high_y, 1.0, 0.0).astype(F32)
    columns = jnp.where(row_at < 32, one, jnp.where(row_at < 36, one * inside_high, one * inside_low)) * (1.0 / 12.0)

    def weights(x, carry):
        total = [None, None]
        inside_x = jnp.logical_and(jnp.logical_or(x >= DEPTH, low_x), jnp.logical_or(x < DEPTH + 16, high_x))
        part = columns * jnp.where(inside_x, 1.0, 0.0).astype(F32)
        k = [kap[x, z] for z in range(2)]
        for z in range(2):
            low = (k[z] + kap[x - 1, z]) * part
            high = (k[z] + kap[x + 1, z]) * part
            wxm[x, z] = low
            wxp[x, z] = high
            before = (k[z] + pltpu.roll(k[z], 1, 0)) * part
            after = (k[z] + pltpu.roll(k[z], 39, 0)) * part
            wym[x, z] = before
            wyp[x, z] = after
            total[z] = (low + high) + (before + after)
        inside = (k[0] + k[1]) * part
        below = (k[0] + jnp.where(pair_at == 0, 0.0, pltpu.roll(k[1], 1, 1))) * part
        above = (k[1] + jnp.where(pair_at == 7, 0.0, pltpu.roll(k[0], 127, 1))) * part
        wzi[x] = inside
        wzm[x] = jnp.where(pair_at == 0, 0.0, below)
        wzp[x] = jnp.where(pair_at == 7, 0.0, above)
        wc[x, 0] = part * 24.0 - (total[0] + (inside + below))
        wc[x, 1] = part * 24.0 - (total[1] + (inside + above))
        return carry

    lax.fori_loop(1, 23, weights, 0)

    most = recv1.at[pl.ds(0, (NDEV - 1) * 16)]
    pltpu.make_async_copy(most, most, tsem.at[1]).wait()

    def forward(quad, carry):
        rows = []
        for i in range(4):
            cells = recv1[pl.ds(quad * 4 + i, 128, stride=16), :].T
            rows.append(jnp.concatenate([cells[:64], cells[64:]], axis=1))
        spectrum = dot(jnp.concatenate(rows, axis=0), dft0[...], dft1[...])
        for i in range(4):
            x = quad * 4 + i
            for z in range(2):
                at = i * 64 + z * 32
                re = spectrum[at : at + 32, 0:128]
                im = spectrum[at : at + 32, 128:256]
                u0[0, DEPTH + x, z, 0:32] = re
                u0[1, DEPTH + x, z, 0:32] = im
                acc[0, x, z] = beta[0, 0:1, :] * re + beta[0, 2:3, :] * im
                acc[1, x, z] = beta[0, 1:2, :] * re + beta[0, 3:4, :] * im
        return carry

    lax.fori_loop(0, 4, forward, 0)

    def swap(block, p, act):
        exchange((u0, u3)[block].at[p], hsend.at[block, p], hrecv.at[block, p], act)

    def chebyshev(block, p):
        begin = (u0, u3)[block]
        for m in range(BLOCK):
            now = (begin, u1, begin, u2)[m]
            old = (None, begin, u1, begin)[m]
            new = (u1, begin, u2, u3)[m]
            last = m == BLOCK - 1
            spare = BLOCK - 1 - m
            h = slice(0, 32 if last else 40)

            def sweep(step, carry, now=now, old=old, new=new, last=last, spare=spare, h=h):
                first = DEPTH - spare + step * UNROLL
                field = [[now[p, first + i, z] for z in range(2)] for i in range(-1, UNROLL + 1)]
                values = []
                for i in range(UNROLL):
                    x = first + i
                    below, mid, above = field[i], field[i + 1], field[i + 2]
                    for z in range(2):
                        other = mid[1 - z][h]
                        outer = pltpu.roll(other, 1 if z == 0 else 127, 1)
                        before = pltpu.roll(mid[z], 1, 0)[h]
                        after = pltpu.roll(mid[z], 39, 0)[h]
                        value = wc[x, z, h] * mid[z][h] + wzi[x, h] * other
                        value = value + (wxm[x, z, h] * below[z][h] + wxp[x, z, h] * above[z][h])
                        if old is not None:
                            value = value - old[p, x, z, h]
                        rest = wym[x, z, h] * before + wyp[x, z, h] * after
                        value = value + (rest + (wzm if z == 0 else wzp)[x, h] * outer)
                        values.append((x, z, mid[z][h], value))
                if last:
                    totals = []
                    for x, z, own, value in values:
                        terms = [u1[p, x, z, h], old[p, x, z, h], own, value]
                        for to in range(2):
                            at = 2 * p + to
                            total = beta[BLOCK * block + 1, at : at + 1, :] * terms[0]
                            for i in range(1, 4):
                                total = total + beta[BLOCK * block + 1 + i, at : at + 1, :] * terms[i]
                            totals.append((to, x, z, acc[to, x - DEPTH, z] + total))
                    for to, x, z, total in totals:
                        acc[to, x - DEPTH, z] = total
                if not last or block == 0:
                    for x, z, own, value in values:
                        new[p, x, z, h] = value
                return carry

            lax.fori_loop(0, (16 + 2 * spare) // UNROLL, sweep, 0)

    swap(0, 0, "start")
    swap(0, 1, "start")
    for block in range(2):
        for p in range(2):
            swap(block, p, "wait")
            chebyshev(block, p)
            if block == 0:
                swap(1, p, "start")

    def inverse(quad, carry):
        rows = []
        for i in range(4):
            x = quad * 4 + i
            rows.append(
                jnp.concatenate([acc[0, x].reshape(64, 128), acc[1, x].reshape(64, 128)], axis=1)
            )
        times = dot(jnp.concatenate(rows, axis=0), back0[...], back1[...])
        for i in range(4):
            own = times[i * 64 : i * 64 + 64]
            cells = jnp.concatenate([own[:, :128], own[:, 128:]], axis=0)
            send2[pl.ds(quad * 4 + i, 128, stride=16), :] = cells.T
        return carry

    lax.fori_loop(0, 4, inverse, 0)

    def t2_go(k, carry):
        kk = (k * 37) % NDEV
        t0 = (tm // 4 + kk // 32) % 4 * 4 + (tm + kk // 8) % 4
        t1 = (sp // 2 + kk // 2) % 4 * 2 + (sp + kk) % 2
        pltpu.make_async_remote_copy(
            src_ref=send2.at[rows16(t0 * NSP + t1)],
            dst_ref=recv2.at[rows16(tile)],
            send_sem=tsem.at[2],
            recv_sem=tsem.at[3],
            device_id=(t0, t1),
            device_id_type=MESH,
        ).start()
        return carry

    lax.fori_loop(1, NDEV, t2_go, 0)
    recv2[rows16(tile), :] = send2[rows16(me), :]
    most2 = recv2.at[pl.ds(0, (NDEV - 1) * 16)]
    pltpu.make_async_copy(most2, most2, tsem.at[3]).wait()

    def unpack(x, carry):
        for xt in range(2):
            rows = pl.ds(pl.multiple_of(x * 16 + xt * 8, 8), 8)
            for h in range(2):
                parts = [
                    recv2[pl.ds(pl.multiple_of((x * 8 + h * 4 + j) * 16 + xt * 8, 8), 8), :]
                    for j in range(4)
                ]
                for i, value in enumerate(swap_groups(parts)):
                    source[i // 2, i % 2, rows, h * 128 : h * 128 + 128] = value * unscales[i // 2]
        rows = pl.ds(pl.multiple_of(x * 16, 16), 16)
        pltpu.make_async_copy(source.at[:, :, rows, :], out.at[:, :, rows, :], outsem).start()
        return carry

    lax.fori_loop(0, 16, unpack, 0)

    pltpu.make_async_copy(most, most, tsem.at[0]).wait()
    pltpu.make_async_copy(most2, most2, tsem.at[2]).wait()
    pltpu.make_async_copy(some, some, tsem.at[4]).wait()
    pltpu.make_async_copy(source, out, outsem).wait()


def body(source, start_field, last_guess, classes, conductivity, alpha_num):
    consts = [jnp.asarray(t) for t in tables()]
    smem = pl.BlockSpec(memory_space=pltpu.SMEM)
    hbm = pl.BlockSpec(memory_space=pltpu.HBM)
    BF16 = jnp.bfloat16
    V = pltpu.VMEM
    return pl.pallas_call(
        kernel,
        out_shape=jax.ShapeDtypeStruct((2, 2, 256, 256), F32),
        in_specs=[smem, smem] + [hbm] * 7,
        out_specs=hbm,
        scratch_shapes=[
            V((2, 2, 256, 256), F32), V((2, 256, 256), F32), V((2, 256, 256), F32), V((2, 32, 128), jnp.int32),
            V((256, 256), F32), V((256, 256), F32), V((256, 256), BF16), V((256, 256), BF16), V((256, 256), BF16), V((256, 256), BF16), V((16, 128), F32),
            pltpu.SemaphoreType.DMA((7,)),
            V((2048, 128), F32), V((2048, 128), F32), V((2048, 128), F32), V((2048, 128), F32),
            V((2, 4, 8, 128), jnp.int32), V((64, 128), jnp.int32),
            V((24, 2, 40, 128), F32), V((24, 2, 40, 128), F32), V((24, 2, 40, 128), F32), V((24, 2, 40, 128), F32),
            V((24, 2, 40, 128), F32),
            V((24, 40, 128), F32), V((24, 40, 128), F32), V((24, 40, 128), F32), V((24, 2, 40, 128), F32),
            V((2, 24, 2, 40, 128), F32), V((2, 24, 2, 40, 128), F32), V((2, 24, 2, 40, 128), F32), V((2, 24, 2, 40, 128), F32), V((2, 16, 2, 32, 128), F32), V((CHEB + 1, 8, 128), F32),
            pltpu.SemaphoreType.DMA((6,)),
            pltpu.SemaphoreType.DMA((8,)), pltpu.SemaphoreType.DMA((8,)),
            pltpu.SemaphoreType.DMA((2, 2, 8)), pltpu.SemaphoreType.DMA((2, 2, 8)), pltpu.SemaphoreType.DMA,
        ],
        compiler_params=pltpu.CompilerParams(
            collective_id=1, has_side_effects=True, vmem_limit_bytes=62 * 2**20
        ),
    )(alpha_num, conductivity, source, start_field, last_guess, classes, *consts)


def solution(mesh):
    placed = (
        P("tm", "space", None, None),
        P("space", None, None),
        P("space", None, None),
        P("space", None, None),
        P(),
        P(),
    )
    return jax.shard_map(
        body, mesh=mesh, in_specs=placed, out_specs=P("tm", "space", None, None), check_vma=False
    )
```

time: 105 us -> 76.8 us (0.73)
  Pallas kernels: 95.8 us -> 73.7 us
  local copies, waits for them, and re-layouts: 7.91 us -> 2.29 us
    pallas_call x1, Pallas kernels: 95.8 us -> 73.7 us  [body(): pl.pallas_call(kernel, out_shape=jax.ShapeDtypeStruct((2, 2, 256, 256), F...]
    unnamed x17 -> x1, local copies, waits for them, and re-layouts: 7.91 us -> 2.29 us
where the time goes in v1:
time: 76.8 us; the launch traced here: 76.6 us
  Pallas kernels  73.7 us (96%)
  local copies, waits for them, and re-layouts  2.29 us (3%)
    pallas_call x1, Pallas kernels, body(): pl.pallas_call(kernel, out_shape=jax.ShapeDtypeStruct((2, 2, 256, 256), F...  73.7 us
    unnamed x1, local copies, waits for them, and re-layouts  2.29 us

profile of v1, /device:TPU:1, one launch (start us, length us, event | category | flops | bytes accessed | tf_op | source)
XLA Modules:
  0.0 76.6 jit_solution(4014342939606991150)
XLA Ops:
  0.7 73.7 %shard_map.91 = f32[2,2,256,256]{3,2,1,0:T(8,128)} custom-call(s32[1]{0:T(128)S(6)} %copy.11.anum, f32[8]{0:T(128)} %cond.1, f32[2,2,256,256]{3,2,1,0:T(8,128)} %source_in.1, f32[2,256,256]{2,1,0:T(8,128)} %start_in.1, f32[2,256,256]{2,1,0:T(8,128)} %guess_in.1, s32[2,256,256]{2,1,0:T(8,128)} %classes_in.1, f32[256,256]{1,0:T(8,128)} %constant.6.clone.dft_in, ...), custom_call_target="tpu_custom_call" | custom-call | tf_op jit(solution)/shard_map/pallas_call | solution.py:539
  74.3 2.3 %copy.12 = f32[2,2,256,256]{3,2,1,0:T(8,128)} copy(f32[2,2,256,256]{3,2,1,0:T(8,128)} %shard_map.91) | data formatting | bytes 2097152

commit v2 on v1

--- a/solution.py
+++ b/solution.py
@@ -15,6 +15,10 @@
 HALF_SPAN = 12.0
 NTM, NSP = 16, 8
 NDEV = NTM * NSP
+OFFSETS = sorted(
+    [(dx, dz, dy, dc) for dx in range(4) for dz in range(4) for dy in range(4) for dc in range(2)][1:],
+    key=lambda o: -sum(min(d, 4 - d) for d in o[:3]),
+)
 DEPTH = 4
 BLOCK = 4
 UNROLL = 2
@@ -149,6 +153,13 @@
     xi, yi = tile_of(tm, sp)
     tile = xi * 8 + yi
 
+    planes = [[(tm // 4 + dx) % 4 * 4 + (tm + dz) % 4 for dz in range(4)] for dx in range(4)]
+    places = [[(sp // 2 + dy) % 4 * 2 + (sp + dc) % 2 for dc in range(2)] for dy in range(4)]
+
+    barrier = pltpu.get_barrier_semaphore()
+    for dx, dz, dy, dc in OFFSETS:
+        pl.semaphore_signal(barrier, inc=1, device_id=(planes[dx][dz], places[dy][dc]), device_id_type=MESH)
+
     zhi = tm % 4 // 2
     half_lanes = pl.ds(pl.multiple_of(zhi * 128, 128), 128)
     pair_rows = pl.ds(pl.multiple_of(xi // 2 * 32, 32), 32)
@@ -172,23 +183,31 @@
         for copy in firsts:
             copy.start()
 
-    barrier = pltpu.get_barrier_semaphore()
-
-    def clear(x, carry):
-        kap[x] = jnp.zeros((2, 40, 128), F32)
-        for p in range(2):
-            u0[p, x] = jnp.zeros((2, 40, 128), F32)
-            u3[p, x] = jnp.zeros((2, 40, 128), F32)
-        return carry
-
-    lax.fori_loop(0, 24, clear, 0)
-
-    def greet(k, carry):
-        t = (me + k) % NDEV
-        pl.semaphore_signal(barrier, inc=1, device_id=(t // NSP, t % NSP), device_id_type=MESH)
-        return carry
-
-    lax.fori_loop(1, NDEV, greet, 0)
+
+    low_x, high_x, low_y, high_y = xi > 0, xi < 15, yi > 0, yi < 7
+    beside = {-1: low_x, 1: high_x}, {-1: low_y, 1: high_y}
+
+    def here(dx, dy):
+        if dx and dy:
+            return jnp.logical_and(beside[0][dx], beside[1][dy])
+        return beside[0][dx] if dx else beside[1][dy]
+
+    def span(d, low, middle, high):
+        return {-1: low, 0: middle, 1: high}[d]
+
+    def halo(dx, dy):
+        return (
+            span(dx, pl.ds(0, DEPTH), pl.ds(DEPTH, 16), pl.ds(DEPTH + 16, DEPTH)),
+            span(dy, pl.ds(36, 4), pl.ds(0, 32), pl.ds(32, 4)),
+        )
+
+    for dx, dy in SIDES:
+
+        @pl.when(jnp.logical_not(here(dx, dy)))
+        def _(dx=dx, dy=dy):
+            xs, ys = halo(dx, dy)
+            for ref in (kap, u0.at[0], u0.at[1], u3.at[0], u3.at[1]):
+                ref[xs, :, ys, :] = jnp.zeros((xs.size, 2, ys.size, 128), F32)
 
     log_alpha = jnp.log(jnp.full((8, 128), anum[0].astype(F32) / 32.0, F32))
     alpha = anum[0].astype(F32) / 32.0
@@ -269,22 +288,18 @@
     def rows16(index):
         return pl.ds(pl.multiple_of(index * 16, 16), 16)
 
-    def t1_go(k, carry):
-        kk = (k * 37) % NDEV
-        t0 = (tm // 4 + kk // 32) % 4 * 4 + (tm + kk // 8) % 4
-        t1 = (sp // 2 + kk // 2) % 4 * 2 + (sp + kk) % 2
-        ox, oy = tile_of(t0, t1)
+    tiles_x = [[tile_of(planes[dx][dz], sp)[0] - sp % 2 for dz in range(4)] for dx in range(4)]
+    tiles_y = [[tile_of(planes[0][dz], places[dy][0])[1] for dz in range(4)] for dy in range(4)]
+    for dx, dz, dy, dc in OFFSETS:
+        other = (tiles_x[dx][dz] + (sp + dc) % 2) * 8 + tiles_y[dy][dz]
         pltpu.make_async_remote_copy(
-            src_ref=send1.at[rows16(ox * 8 + oy)],
+            src_ref=send1.at[rows16(other)],
             dst_ref=recv1.at[rows16(me)],
             send_sem=tsem.at[0],
             recv_sem=tsem.at[1],
-            device_id=(t0, t1),
+            device_id=(planes[dx][dz], places[dy][dc]),
             device_id_type=MESH,
         ).start()
-        return carry
-
-    lax.fori_loop(1, NDEV, t1_go, 0)
     recv1[rows16(me), :] = send1[rows16(tile), :]
     mycy, mycore = sp // 2, sp % 2
     cls_recv[pl.ds(pl.multiple_of(sp * 8, 8), 8), :] = cls_send[mycore, mycy + zhi * (3 - 2 * mycy)]
@@ -303,23 +318,6 @@
         return carry
 
     lax.fori_loop(0, 8, conductivities, 0)
-
-    low_x, high_x, low_y, high_y = xi > 0, xi < 15, yi > 0, yi < 7
-    beside = {-1: low_x, 1: high_x}, {-1: low_y, 1: high_y}
-
-    def here(dx, dy):
-        if dx and dy:
-            return jnp.logical_and(beside[0][dx], beside[1][dy])
-        return beside[0][dx] if dx else beside[1][dy]
-
-    def span(d, low, middle, high):
-        return {-1: low, 0: middle, 1: high}[d]
-
-    def halo(dx, dy):
-        return (
-            span(dx, pl.ds(0, DEPTH), pl.ds(DEPTH, 16), pl.ds(DEPTH + 16, DEPTH)),
-            span(dy, pl.ds(36, 4), pl.ds(0, 32), pl.ds(32, 4)),
-        )
 
     def edge(dx, dy):
         return (
@@ -354,42 +352,6 @@
                     pltpu.make_async_copy(got, got, recv.at[i]).wait()
 
     exchange(kap, ksend, krecv, "start")
-    exchange(kap, ksend, krecv, "wait")
-
-    row_at = lax.broadcasted_iota(jnp.int32, (40, 128), 0)
-    pair_at = lax.broadcasted_iota(jnp.int32, (40, 128), 1) % 8
-    one = jnp.ones((40, 128), F32)
-    inside_low = jnp.where(low_y, 1.0, 0.0).astype(F32)
-    inside_high = jnp.where(high_y, 1.0, 0.0).astype(F32)
-    columns = jnp.where(row_at < 32, one, jnp.where(row_at < 36, one * inside_high, one * inside_low)) * (1.0 / 12.0)
-
-    def weights(x, carry):
-        total = [None, None]
-        inside_x = jnp.logical_and(jnp.logical_or(x >= DEPTH, low_x), jnp.logical_or(x < DEPTH + 16, high_x))
-        part = columns * jnp.where(inside_x, 1.0, 0.0).astype(F32)
-        k = [kap[x, z] for z in range(2)]
-        for z in range(2):
-            low = (k[z] + kap[x - 1, z]) * part
-            high = (k[z] + kap[x + 1, z]) * part
-            wxm[x, z] = low
-            wxp[x, z] = high
-            before = (k[z] + pltpu.roll(k[z], 1, 0)) * part
-            after = (k[z] + pltpu.roll(k[z], 39, 0)) * part
-            wym[x, z] = before
-            wyp[x, z] = after
-            total[z] = (low + high) + (before + after)
-        inside = (k[0] + k[1]) * part
-        below = (k[0] + jnp.where(pair_at == 0, 0.0, pltpu.roll(k[1], 1, 1))) * part
-        above = (k[1] + jnp.where(pair_at == 7, 0.0, pltpu.roll(k[0], 127, 1))) * part
-        wzi[x] = inside
-        wzm[x] = jnp.where(pair_at == 0, 0.0, below)
-        wzp[x] = jnp.where(pair_at == 7, 0.0, above)
-        wc[x, 0] = part * 24.0 - (total[0] + (inside + below))
-        wc[x, 1] = part * 24.0 - (total[1] + (inside + above))
-        return carry
-
-    lax.fori_loop(1, 23, weights, 0)
-
     most = recv1.at[pl.ds(0, (NDEV - 1) * 16)]
     pltpu.make_async_copy(most, most, tsem.at[1]).wait()
 
@@ -466,6 +428,42 @@
 
     swap(0, 0, "start")
     swap(0, 1, "start")
+    exchange(kap, ksend, krecv, "wait")
+
+    row_at = lax.broadcasted_iota(jnp.int32, (40, 128), 0)
+    pair_at = lax.broadcasted_iota(jnp.int32, (40, 128), 1) % 8
+    one = jnp.ones((40, 128), F32)
+    inside_low = jnp.where(low_y, 1.0, 0.0).astype(F32)
+    inside_high = jnp.where(high_y, 1.0, 0.0).astype(F32)
+    columns = jnp.where(row_at < 32, one, jnp.where(row_at < 36, one * inside_high, one * inside_low)) * (1.0 / 12.0)
+
+    def weights(x, carry):
+        total = [None, None]
+        inside_x = jnp.logical_and(jnp.logical_or(x >= DEPTH, low_x), jnp.logical_or(x < DEPTH + 16, high_x))
+        part = columns * jnp.where(inside_x, 1.0, 0.0).astype(F32)
+        k = [kap[x, z] for z in range(2)]
+        for z in range(2):
+            low = (k[z] + kap[x - 1, z]) * part
+            high = (k[z] + kap[x + 1, z]) * part
+            wxm[x, z] = low
+            wxp[x, z] = high
+            before = (k[z] + pltpu.roll(k[z], 1, 0)) * part
+            after = (k[z] + pltpu.roll(k[z], 39, 0)) * part
+            wym[x, z] = before
+            wyp[x, z] = after
+            total[z] = (low + high) + (before + after)
+        inside = (k[0] + k[1]) * part
+        below = (k[0] + jnp.where(pair_at == 0, 0.0, pltpu.roll(k[1], 1, 1))) * part
+        above = (k[1] + jnp.where(pair_at == 7, 0.0, pltpu.roll(k[0], 127, 1))) * part
+        wzi[x] = inside
+        wzm[x] = jnp.where(pair_at == 0, 0.0, below)
+        wzp[x] = jnp.where(pair_at == 7, 0.0, above)
+        wc[x, 0] = part * 24.0 - (total[0] + (inside + below))
+        wc[x, 1] = part * 24.0 - (total[1] + (inside + above))
+        return carry
+
+    lax.fori_loop(1, 23, weights, 0)
+
     for block in range(2):
         for p in range(2):
             swap(block, p, "wait")
@@ -489,21 +487,15 @@
 
     lax.fori_loop(0, 4, inverse, 0)
 
-    def t2_go(k, carry):
-        kk = (k * 37) % NDEV
-        t0 = (tm // 4 + kk // 32) % 4 * 4 + (tm + kk // 8) % 4
-        t1 = (sp // 2 + kk // 2) % 4 * 2 + (sp + kk) % 2
+    for dx, dz, dy, dc in OFFSETS:
         pltpu.make_async_remote_copy(
-            src_ref=send2.at[rows16(t0 * NSP + t1)],
+            src_ref=send2.at[rows16(planes[dx][dz] * NSP + places[dy][dc])],
             dst_ref=recv2.at[rows16(tile)],
             send_sem=tsem.at[2],
             recv_sem=tsem.at[3],
-            device_id=(t0, t1),
+            device_id=(planes[dx][dz], places[dy][dc]),
             device_id_type=MESH,
         ).start()
-        return carry
-
-    lax.fori_loop(1, NDEV, t2_go, 0)
     recv2[rows16(tile), :] = send2[rows16(me), :]
     most2 = recv2.at[pl.ds(0, (NDEV - 1) * 16)]
     pltpu.make_async_copy(most2, most2, tsem.at[3]).wait()

time: 76.8 us -> 70.3 us (0.915)
  Pallas kernels: 73.7 us -> 67.2 us
    pallas_call x1, Pallas kernels: 73.7 us -> 67.2 us  [body(): pl.pallas_call(kernel, out_shape=jax.ShapeDtypeStruct((2, 2, 256, 256), F...]
where the time goes in v2:
time: 70.3 us; the launch traced here: 70.1 us
  Pallas kernels  67.2 us (96%)
  local copies, waits for them, and re-layouts  2.29 us (3%)
    pallas_call x1, Pallas kernels, body(): pl.pallas_call(kernel, out_shape=jax.ShapeDtypeStruct((2, 2, 256, 256), F...  67.2 us
    unnamed x1, local copies, waits for them, and re-layouts  2.29 us

profile of v2, /device:TPU:1, one launch (start us, length us, event | category | flops | bytes accessed | tf_op | source)
XLA Modules:
  0.0 70.1 jit_solution(1391657685431380645)
XLA Ops:
  0.7 67.2 %shard_map.91 = f32[2,2,256,256]{3,2,1,0:T(8,128)} custom-call(s32[1]{0:T(128)S(6)} %copy.11.anum, f32[8]{0:T(128)} %cond.1, f32[2,2,256,256]{3,2,1,0:T(8,128)} %source_in.1, f32[2,256,256]{2,1,0:T(8,128)} %start_in.1, f32[2,256,256]{2,1,0:T(8,128)} %guess_in.1, s32[2,256,256]{2,1,0:T(8,128)} %classes_in.1, f32[256,256]{1,0:T(8,128)} %constant.6.clone.dft_in, ...), custom_call_target="tpu_custom_call" | custom-call | tf_op jit(solution)/shard_map/pallas_call | solution.py:531
  67.8 2.3 %copy.12 = f32[2,2,256,256]{3,2,1,0:T(8,128)} copy(f32[2,2,256,256]{3,2,1,0:T(8,128)} %shard_map.91) | data formatting | bytes 2097152

commit v3 on v2

--- a/solution.py
+++ b/solution.py
@@ -21,7 +21,7 @@
 )
 DEPTH = 4
 BLOCK = 4
-UNROLL = 2
+UNROLL = 8
 SIDES = [(dx, dy) for dx in (-1, 0, 1) for dy in (-1, 0, 1) if (dx, dy) != (0, 0)]
 
 
@@ -143,9 +143,9 @@
 
 
 def kernel(
-    anum, cond, source_in, start_in, guess_in, classes_in, dft_in, back_in, trig_in, out,
-    source, start, guess, classes, dft, back, dft0, dft1, back0, back1, trig, insem, send1, recv1, send2, recv2, cls_send, cls_recv, kap, wxm, wxp, wym, wyp, wzi, wzm, wzp, wc,
-    u0, u1, u2, u3, acc, beta, tsem, ksend, krecv, hsend, hrecv, outsem,
+    anum, cond, source_in, start_in, guess_in, classes_in, dft_in, back_in, trig_in, recv2,
+    source, start, guess, classes, dft, back, dft0, dft1, back0, back1, trig, insem, send1, recv1, send2, cls_send, cls_recv, kap, wxm, wxp, wym, wyp, wzi, wzm, wzp, wc,
+    u0, u1, u2, u3, acc, beta, tsem, ksend, krecv, hsend, hrecv, selfsem,
 ):
     tm = lax.axis_index("tm")
     sp = lax.axis_index("space")
@@ -155,10 +155,6 @@
 
     planes = [[(tm // 4 + dx) % 4 * 4 + (tm + dz) % 4 for dz in range(4)] for dx in range(4)]
     places = [[(sp // 2 + dy) % 4 * 2 + (sp + dc) % 2 for dc in range(2)] for dy in range(4)]
-
-    barrier = pltpu.get_barrier_semaphore()
-    for dx, dz, dy, dc in OFFSETS:
-        pl.semaphore_signal(barrier, inc=1, device_id=(planes[dx][dz], places[dy][dc]), device_id_type=MESH)
 
     zhi = tm % 4 // 2
     half_lanes = pl.ds(pl.multiple_of(zhi * 128, 128), 128)
@@ -184,6 +180,10 @@
             copy.start()
 
 
+    barrier = pltpu.get_barrier_semaphore()
+    for dx, dz, dy, dc in OFFSETS:
+        pl.semaphore_signal(barrier, inc=1, device_id=(planes[dx][dz], places[dy][dc]), device_id_type=MESH)
+
     low_x, high_x, low_y, high_y = xi > 0, xi < 15, yi > 0, yi < 7
     beside = {-1: low_x, 1: high_x}, {-1: low_y, 1: high_y}
 
@@ -201,29 +201,10 @@
             span(dy, pl.ds(36, 4), pl.ds(0, 32), pl.ds(32, 4)),
         )
 
-    for dx, dy in SIDES:
-
-        @pl.when(jnp.logical_not(here(dx, dy)))
-        def _(dx=dx, dy=dy):
-            xs, ys = halo(dx, dy)
-            for ref in (kap, u0.at[0], u0.at[1], u3.at[0], u3.at[1]):
-                ref[xs, :, ys, :] = jnp.zeros((xs.size, 2, ys.size, 128), F32)
-
     log_alpha = jnp.log(jnp.full((8, 128), anum[0].astype(F32) / 32.0, F32))
     alpha = anum[0].astype(F32) / 32.0
     n0 = (2 * tm).astype(F32)
     scales = [jnp.exp(log_alpha * (n0 + t) / STEPS) for t in range(2)]
-    unscales = [jnp.exp(-log_alpha * (n0 + t) / STEPS) for t in range(2)]
-
-    loads[1].wait()
-    for core in range(2):
-        parts = [
-            classes[z, core * 16 + xt * 8 : core * 16 + xt * 8 + 8, :]
-            for xt in range(2)
-            for z in range(2)
-        ]
-        for j, value in enumerate(swap_groups(parts)):
-            cls_send[core, j] = value
 
     loads[0].wait()
 
@@ -240,8 +221,9 @@
 
         lax.fori_loop(0, 16, correct, 0)
 
-    def pack(x, carry):
-        for xt in range(2):
+    def pack(step, carry):
+        todo = []
+        for x, xt in [(2 * step + i, xt) for i in range(2) for xt in range(2)]:
             rows = pl.ds(pl.multiple_of(x * 16 + xt * 8, 8), 8)
             for h in range(2):
                 lanes = slice(h * 128, h * 128 + 128)
@@ -252,20 +234,22 @@
                         parts.append(value * scales[t])
                 for j, value in enumerate(swap_groups(parts)):
                     at = pl.multiple_of((x * 8 + h * 4 + j) * 16 + xt * 8, 8)
-                    send1[pl.ds(at, 8), :] = value
+                    todo.append((at, value))
+        for at, value in todo:
+            send1[pl.ds(at, 8), :] = value
         return carry
 
-    lax.fori_loop(0, 16, pack, 0)
-
-    for copy in loads[2:]:
-        copy.wait()
-    dft0[...], dft1[...] = two_terms(dft[...])
-    back0[...], back1[...] = two_terms(back[...])
-    for j, (re, im) in enumerate(chebyshev_table(log_alpha, trig[0:8, :], trig[8:16, :])):
-        beta[j, 0:1, :] = re[0:1]
-        beta[j, 1:2, :] = im[0:1]
-        beta[j, 2:3, :] = -im[0:1]
-        beta[j, 3:4, :] = re[4:5]
+    lax.fori_loop(0, 8, pack, 0)
+
+    loads[1].wait()
+    for core in range(2):
+        parts = [
+            classes[z, core * 16 + xt * 8 : core * 16 + xt * 8 + 8, :]
+            for xt in range(2)
+            for z in range(2)
+        ]
+        for j, value in enumerate(swap_groups(parts)):
+            cls_send[core, j] = value
 
     pl.semaphore_wait(barrier, NDEV - 1)
 
@@ -303,6 +287,24 @@
     recv1[rows16(me), :] = send1[rows16(tile), :]
     mycy, mycore = sp // 2, sp % 2
     cls_recv[pl.ds(pl.multiple_of(sp * 8, 8), 8), :] = cls_send[mycore, mycy + zhi * (3 - 2 * mycy)]
+
+    for copy in loads[2:]:
+        copy.wait()
+    dft0[...], dft1[...] = two_terms(dft[...])
+    back0[...], back1[...] = two_terms(back[...])
+    for j, (re, im) in enumerate(chebyshev_table(log_alpha, trig[0:8, :], trig[8:16, :])):
+        beta[j, 0:1, :] = re[0:1]
+        beta[j, 1:2, :] = im[0:1]
+        beta[j, 2:3, :] = -im[0:1]
+        beta[j, 3:4, :] = re[4:5]
+
+    for dx, dy in SIDES:
+
+        @pl.when(jnp.logical_not(here(dx, dy)))
+        def _(dx=dx, dy=dy):
+            xs, ys = halo(dx, dy)
+            for ref in (kap, u0.at[0], u0.at[1], u3.at[0], u3.at[1]):
+                ref[xs, :, ys, :] = jnp.zeros((xs.size, 2, ys.size, 128), F32)
 
     some = cls_recv.at[pl.ds(0, 56)]
     pltpu.make_async_copy(some, some, tsem.at[5]).wait()
@@ -388,11 +390,10 @@
             spare = BLOCK - 1 - m
             h = slice(0, 32 if last else 40)
 
-            def sweep(step, carry, now=now, old=old, new=new, last=last, spare=spare, h=h):
-                first = DEPTH - spare + step * UNROLL
-                field = [[now[p, first + i, z] for z in range(2)] for i in range(-1, UNROLL + 1)]
+            def sweep(first, count, now=now, old=old, new=new, last=last, h=h):
+                field = [[now[p, first + i, z] for z in range(2)] for i in range(-1, count + 1)]
                 values = []
-                for i in range(UNROLL):
+                for i in range(count):
                     x = first + i
                     below, mid, above = field[i], field[i + 1], field[i + 2]
                     for z in range(2):
@@ -422,9 +423,16 @@
                 if not last or block == 0:
                     for x, z, own, value in values:
                         new[p, x, z, h] = value
+
+            steps, rest = divmod(16 + 2 * spare, UNROLL)
+
+            def several(step, carry, sweep=sweep, spare=spare):
+                sweep(DEPTH - spare + step * UNROLL, UNROLL)
                 return carry
 
-            lax.fori_loop(0, (16 + 2 * spare) // UNROLL, sweep, 0)
+            lax.fori_loop(0, steps, several, 0)
+            if rest:
+                sweep(DEPTH - spare + steps * UNROLL, rest)
 
     swap(0, 0, "start")
     swap(0, 1, "start")
@@ -496,30 +504,31 @@
             device_id=(planes[dx][dz], places[dy][dc]),
             device_id_type=MESH,
         ).start()
-    recv2[rows16(tile), :] = send2[rows16(me), :]
+    own = pltpu.make_async_copy(send2.at[rows16(me)], recv2.at[rows16(tile)], selfsem)
+    own.start()
+    own.wait()
     most2 = recv2.at[pl.ds(0, (NDEV - 1) * 16)]
     pltpu.make_async_copy(most2, most2, tsem.at[3]).wait()
-
-    def unpack(x, carry):
-        for xt in range(2):
-            rows = pl.ds(pl.multiple_of(x * 16 + xt * 8, 8), 8)
-            for h in range(2):
-                parts = [
-                    recv2[pl.ds(pl.multiple_of((x * 8 + h * 4 + j) * 16 + xt * 8, 8), 8), :]
-                    for j in range(4)
-                ]
-                for i, value in enumerate(swap_groups(parts)):
-                    source[i // 2, i % 2, rows, h * 128 : h * 128 + 128] = value * unscales[i // 2]
-        rows = pl.ds(pl.multiple_of(x * 16, 16), 16)
-        pltpu.make_async_copy(source.at[:, :, rows, :], out.at[:, :, rows, :], outsem).start()
-        return carry
-
-    lax.fori_loop(0, 16, unpack, 0)
 
     pltpu.make_async_copy(most, most, tsem.at[0]).wait()
     pltpu.make_async_copy(most2, most2, tsem.at[2]).wait()
     pltpu.make_async_copy(some, some, tsem.at[4]).wait()
-    pltpu.make_async_copy(source, out, outsem).wait()
+
+
+def unpack_kernel(anum, tiles, out):
+    log_alpha = jnp.log(jnp.full((8, 128), anum[0].astype(F32) / 32.0, F32))
+    n0 = (2 * lax.axis_index("tm")).astype(F32)
+    unscales = [jnp.exp(-log_alpha * (n0 + t) / STEPS) for t in range(2)]
+    for x in range(out.shape[2] // 16):
+        todo = []
+        for xt in range(2):
+            row = x * 16 + xt * 8
+            for h in range(2):
+                parts = [tiles[(x * 8 + h * 4 + j) * 16 + xt * 8 : (x * 8 + h * 4 + j) * 16 + xt * 8 + 8, :] for j in range(4)]
+                for i, value in enumerate(swap_groups(parts)):
+                    todo.append((i // 2, i % 2, row, h * 128, value * unscales[i // 2]))
+        for t, z, row, lane, value in todo:
+            out[t, z, row : row + 8, lane : lane + 128] = value
 
 
 def body(source, start_field, last_guess, classes, conductivity, alpha_num):
@@ -528,16 +537,16 @@
     hbm = pl.BlockSpec(memory_space=pltpu.HBM)
     BF16 = jnp.bfloat16
     V = pltpu.VMEM
-    return pl.pallas_call(
+    tiles = pl.pallas_call(
         kernel,
-        out_shape=jax.ShapeDtypeStruct((2, 2, 256, 256), F32),
+        out_shape=jax.ShapeDtypeStruct((2048, 128), F32),
         in_specs=[smem, smem] + [hbm] * 7,
         out_specs=hbm,
         scratch_shapes=[
             V((2, 2, 256, 256), F32), V((2, 256, 256), F32), V((2, 256, 256), F32), V((2, 32, 128), jnp.int32),
             V((256, 256), F32), V((256, 256), F32), V((256, 256), BF16), V((256, 256), BF16), V((256, 256), BF16), V((256, 256), BF16), V((16, 128), F32),
             pltpu.SemaphoreType.DMA((7,)),
-            V((2048, 128), F32), V((2048, 128), F32), V((2048, 128), F32), V((2048, 128), F32),
+            V((2048, 128), F32), V((2048, 128), F32), V((2048, 128), F32),
             V((2, 4, 8, 128), jnp.int32), V((64, 128), jnp.int32),
             V((24, 2, 40, 128), F32), V((24, 2, 40, 128), F32), V((24, 2, 40, 128), F32), V((24, 2, 40, 128), F32),
             V((24, 2, 40, 128), F32),
@@ -551,6 +560,14 @@
             collective_id=1, has_side_effects=True, vmem_limit_bytes=62 * 2**20
         ),
     )(alpha_num, conductivity, source, start_field, last_guess, classes, *consts)
+    steps = 4
+    return pl.pallas_call(
+        unpack_kernel,
+        grid=(steps,),
+        out_shape=jax.ShapeDtypeStruct((2, 2, 256, 256), F32),
+        in_specs=[smem, pl.BlockSpec((2048 // steps, 128), lambda i: (i, 0))],
+        out_specs=pl.BlockSpec((2, 2, 256 // steps, 256), lambda i: (0, 0, i, 0)),
+    )(alpha_num, tiles)
 
 
 def solution(mesh):

time: 70.3 us -> 64.7 us (0.920)
  Pallas kernels: 67.2 us -> 63.8 us
  local copies, waits for them, and re-layouts: 2.29 us -> 0 us
    pallas_call x1 -> x2, Pallas kernels: 67.2 us -> 63.8 us  [the longest x1 60 us: body(): pl.pallas_call(kernel, out_shape=jax.ShapeDtypeStruct((2048, 128), F32),...]
    unnamed x1 -> x0, local copies, waits for them, and re-layouts: 2.29 us -> none
where the time goes in v3:
time: 64.7 us; the launch traced here: 64.5 us
  Pallas kernels  63.8 us (99%)
  between operations  0.66 us (1%)
    pallas_call x1, Pallas kernels, body(): pl.pallas_call(kernel, out_shape=jax.ShapeDtypeStruct((2048, 128), F32),...  60 us
    pallas_call x1, Pallas kernels, body(): pl.pallas_call(unpack_kernel, grid=(steps,), out_shape=jax.ShapeDtypeStru...  3.86 us

profile of v3, /device:TPU:1, one launch (start us, length us, event | category | flops | bytes accessed | tf_op | source)
XLA Modules:
  0.0 64.5 jit_solution(15894648361166411143)
XLA Ops:
  0.7 60.0 %shard_map.91.tiles = f32[2048,128]{1,0:T(8,128)} custom-call(s32[1]{0:T(128)S(6)} %copy.10.anum, f32[8]{0:T(128)} %cond.1, f32[2,2,256,256]{3,2,1,0:T(8,128)} %source_in.1, f32[2,256,256]{2,1,0:T(8,128)} %start_in.1, f32[2,256,256]{2,1,0:T(8,128)} %guess_in.1, s32[2,256,256]{2,1,0:T(8,128)} %classes_in.1, f32[256,256]{1,0:T(8,128)} %constant.6.clone.dft_in, ...), custom_call_target="tpu_custom_call" | custom-call | tf_op jit(solution)/shard_map/pallas_call | solution.py:540
  60.6 3.9 %shard_map.92 = f32[2,2,256,256]{3,2,1,0:T(8,128)} custom-call(s32[1]{0:T(128)S(6)} %copy.10.anum, f32[2048,128]{1,0:T(8,128)} %shard_map.91.tiles), custom_call_target="tpu_custom_call" | custom-call | tf_op jit(solution)/shard_map/pallas_call | solution.py:564

commit v4 on v3

--- a/solution.py
+++ b/solution.py
@@ -144,7 +144,7 @@
 
 def kernel(
     anum, cond, source_in, start_in, guess_in, classes_in, dft_in, back_in, trig_in, recv2,
-    source, start, guess, classes, dft, back, dft0, dft1, back0, back1, trig, insem, send1, recv1, send2, cls_send, cls_recv, kap, wxm, wxp, wym, wyp, wzi, wzm, wzp, wc,
+    source, start, guess, classes, dft, back, dft0, dft1, back0, back1, trig, insem, send1, recv1, send2a, send2b, cls_send, cls_recv, kap, wxm, wxp, wym, wyp, wzi, wzm, wzp, wc,
     u0, u1, u2, u3, acc, beta, tsem, ksend, krecv, hsend, hrecv, selfsem,
 ):
     tm = lax.axis_index("tm")
@@ -223,7 +223,7 @@
 
     def pack(step, carry):
         todo = []
-        for x, xt in [(2 * step + i, xt) for i in range(2) for xt in range(2)]:
+        for x, xt in [(4 * step + i, xt) for i in range(4) for xt in range(2)]:
             rows = pl.ds(pl.multiple_of(x * 16 + xt * 8, 8), 8)
             for h in range(2):
                 lanes = slice(h * 128, h * 128 + 128)
@@ -239,7 +239,7 @@
             send1[pl.ds(at, 8), :] = value
         return carry
 
-    lax.fori_loop(0, 8, pack, 0)
+    lax.fori_loop(0, 4, pack, 0)
 
     loads[1].wait()
     for core in range(2):
@@ -380,7 +380,7 @@
     def swap(block, p, act):
         exchange((u0, u3)[block].at[p], hsend.at[block, p], hrecv.at[block, p], act)
 
-    def chebyshev(block, p):
+    def chebyshev(block, p, half=None):
         begin = (u0, u3)[block]
         for m in range(BLOCK):
             now = (begin, u1, begin, u2)[m]
@@ -424,15 +424,20 @@
                     for x, z, own, value in values:
                         new[p, x, z, h] = value
 
-            steps, rest = divmod(16 + 2 * spare, UNROLL)
-
-            def several(step, carry, sweep=sweep, spare=spare):
-                sweep(DEPTH - spare + step * UNROLL, UNROLL)
+            begin_at = DEPTH + 8 + spare if half == 1 else DEPTH - spare
+            end_at = DEPTH + 8 + spare if half == 0 else DEPTH + 16 + spare
+            steps, rest = divmod(end_at - begin_at, UNROLL)
+
+            def several(step, carry, sweep=sweep, begin_at=begin_at):
+                sweep(begin_at + step * UNROLL, UNROLL)
                 return carry
 
-            lax.fori_loop(0, steps, several, 0)
+            if steps > 1:
+                lax.fori_loop(0, steps, several, 0)
+            else:
+                several(0, 0)
             if rest:
-                sweep(DEPTH - spare + steps * UNROLL, rest)
+                sweep(begin_at + steps * UNROLL, rest)
 
     swap(0, 0, "start")
     swap(0, 1, "start")
@@ -472,14 +477,12 @@
 
     lax.fori_loop(1, 23, weights, 0)
 
-    for block in range(2):
-        for p in range(2):
-            swap(block, p, "wait")
-            chebyshev(block, p)
-            if block == 0:
-                swap(1, p, "start")
-
-    def inverse(quad, carry):
+    for p in range(2):
+        swap(0, p, "wait")
+        chebyshev(0, p)
+        swap(1, p, "start")
+
+    def inverse(quad):
         rows = []
         for i in range(4):
             x = quad * 4 + i
@@ -487,27 +490,37 @@
                 jnp.concatenate([acc[0, x].reshape(64, 128), acc[1, x].reshape(64, 128)], axis=1)
             )
         times = dot(jnp.concatenate(rows, axis=0), back0[...], back1[...])
+        half_out = send2a if quad < 2 else send2b
         for i in range(4):
             own = times[i * 64 : i * 64 + 64]
             cells = jnp.concatenate([own[:, :128], own[:, 128:]], axis=0)
-            send2[pl.ds(quad * 4 + i, 128, stride=16), :] = cells.T
-        return carry
-
-    lax.fori_loop(0, 4, inverse, 0)
-
-    for dx, dz, dy, dc in OFFSETS:
-        pltpu.make_async_remote_copy(
-            src_ref=send2.at[rows16(planes[dx][dz] * NSP + places[dy][dc])],
-            dst_ref=recv2.at[rows16(tile)],
-            send_sem=tsem.at[2],
-            recv_sem=tsem.at[3],
-            device_id=(planes[dx][dz], places[dy][dc]),
-            device_id_type=MESH,
-        ).start()
-    own = pltpu.make_async_copy(send2.at[rows16(me)], recv2.at[rows16(tile)], selfsem)
-    own.start()
-    own.wait()
+            half_out[pl.ds(quad % 2 * 4 + i, 128, stride=8), :] = cells.T
+
+    kept = []
+    for half, half_out in enumerate((send2a, send2b)):
+        for p in range(2):
+            if half == 0:
+                swap(1, p, "wait")
+            chebyshev(1, p, half)
+        inverse(2 * half)
+        inverse(2 * half + 1)
+        mine = pl.ds(pl.multiple_of(tile * 16 + half * 8, 8), 8)
+        for dx, dz, dy, dc in OFFSETS:
+            to = planes[dx][dz] * NSP + places[dy][dc]
+            pltpu.make_async_remote_copy(
+                src_ref=half_out.at[pl.ds(pl.multiple_of(to * 8, 8), 8)],
+                dst_ref=recv2.at[mine],
+                send_sem=tsem.at[2],
+                recv_sem=tsem.at[3],
+                device_id=(planes[dx][dz], places[dy][dc]),
+                device_id_type=MESH,
+            ).start()
+        stays = pltpu.make_async_copy(half_out.at[pl.ds(pl.multiple_of(me * 8, 8), 8)], recv2.at[mine], selfsem.at[half])
+        stays.start()
+        kept.append(stays)
     most2 = recv2.at[pl.ds(0, (NDEV - 1) * 16)]
+    for stays in kept:
+        stays.wait()
     pltpu.make_async_copy(most2, most2, tsem.at[3]).wait()
 
     pltpu.make_async_copy(most, most, tsem.at[0]).wait()
@@ -519,16 +532,22 @@
     log_alpha = jnp.log(jnp.full((8, 128), anum[0].astype(F32) / 32.0, F32))
     n0 = (2 * lax.axis_index("tm")).astype(F32)
     unscales = [jnp.exp(-log_alpha * (n0 + t) / STEPS) for t in range(2)]
-    for x in range(out.shape[2] // 16):
+
+    def pair(step, carry):
         todo = []
-        for xt in range(2):
-            row = x * 16 + xt * 8
+        for x, xt in [(2 * step + i, xt) for i in range(2) for xt in range(2)]:
+            row = pl.multiple_of(x * 16 + xt * 8, 8)
             for h in range(2):
-                parts = [tiles[(x * 8 + h * 4 + j) * 16 + xt * 8 : (x * 8 + h * 4 + j) * 16 + xt * 8 + 8, :] for j in range(4)]
+                parts = [
+                    tiles[pl.ds(pl.multiple_of((x * 8 + h * 4 + j) * 16 + xt * 8, 8), 8), :] for j in range(4)
+                ]
                 for i, value in enumerate(swap_groups(parts)):
                     todo.append((i // 2, i % 2, row, h * 128, value * unscales[i // 2]))
         for t, z, row, lane, value in todo:
-            out[t, z, row : row + 8, lane : lane + 128] = value
+            out[t, z, pl.ds(row, 8), lane : lane + 128] = value
+        return carry
+
+    lax.fori_loop(0, out.shape[2] // 32, pair, 0)
 
 
 def body(source, start_field, last_guess, classes, conductivity, alpha_num):
@@ -546,7 +565,7 @@
             V((2, 2, 256, 256), F32), V((2, 256, 256), F32), V((2, 256, 256), F32), V((2, 32, 128), jnp.int32),
             V((256, 256), F32), V((256, 256), F32), V((256, 256), BF16), V((256, 256), BF16), V((256, 256), BF16), V((256, 256), BF16), V((16, 128), F32),
             pltpu.SemaphoreType.DMA((7,)),
-            V((2048, 128), F32), V((2048, 128), F32), V((2048, 128), F32),
+            V((2048, 128), F32), V((2048, 128), F32), V((1024, 128), F32), V((1024, 128), F32),
             V((2, 4, 8, 128), jnp.int32), V((64, 128), jnp.int32),
             V((24, 2, 40, 128), F32), V((24, 2, 40, 128), F32), V((24, 2, 40, 128), F32), V((24, 2, 40, 128), F32),
             V((24, 2, 40, 128), F32),
@@ -554,13 +573,13 @@
             V((2, 24, 2, 40, 128), F32), V((2, 24, 2, 40, 128), F32), V((2, 24, 2, 40, 128), F32), V((2, 24, 2, 40, 128), F32), V((2, 16, 2, 32, 128), F32), V((CHEB + 1, 8, 128), F32),
             pltpu.SemaphoreType.DMA((6,)),
             pltpu.SemaphoreType.DMA((8,)), pltpu.SemaphoreType.DMA((8,)),
-            pltpu.SemaphoreType.DMA((2, 2, 8)), pltpu.SemaphoreType.DMA((2, 2, 8)), pltpu.SemaphoreType.DMA,
+            pltpu.SemaphoreType.DMA((2, 2, 8)), pltpu.SemaphoreType.DMA((2, 2, 8)), pltpu.SemaphoreType.DMA((2,)),
         ],
         compiler_params=pltpu.CompilerParams(
             collective_id=1, has_side_effects=True, vmem_limit_bytes=62 * 2**20
         ),
     )(alpha_num, conductivity, source, start_field, last_guess, classes, *consts)
-    steps = 4
+    steps = 2
     return pl.pallas_call(
         unpack_kernel,
         grid=(steps,),

time: 64.7 us -> 62.9 us (0.972)
  Pallas kernels: 63.8 us -> 62.1 us
    pallas_call x1, Pallas kernels: 60 us -> 58.8 us  [body(): pl.pallas_call(kernel, out_shape=jax.ShapeDtypeStruct((2048, 128), F32),...]
where the time goes in v4:
time: 62.9 us; the launch traced here: 62.7 us
  Pallas kernels  62.1 us (99%)
  between operations  0.66 us (1%)
    pallas_call x1, Pallas kernels, body(): pl.pallas_call(kernel, out_shape=jax.ShapeDtypeStruct((2048, 128), F32),...  58.8 us
    pallas_call x1, Pallas kernels, body(): pl.pallas_call(unpack_kernel, grid=(steps,), out_shape=jax.ShapeDtypeStru...  3.29 us

profile of v4, /device:TPU:1, one launch (start us, length us, event | category | flops | bytes accessed | tf_op | source)
XLA Modules:
  0.0 62.7 jit_solution(4387569890444064419)
XLA Ops:
  0.7 58.8 %shard_map.91.tiles = f32[2048,128]{1,0:T(8,128)} custom-call(s32[1]{0:T(128)S(6)} %copy.10.anum, f32[8]{0:T(128)} %cond.1, f32[2,2,256,256]{3,2,1,0:T(8,128)} %source_in.1, f32[2,256,256]{2,1,0:T(8,128)} %start_in.1, f32[2,256,256]{2,1,0:T(8,128)} %guess_in.1, s32[2,256,256]{2,1,0:T(8,128)} %classes_in.1, f32[256,256]{1,0:T(8,128)} %constant.6.clone.dft_in, ...), custom_call_target="tpu_custom_call" | custom-call | tf_op jit(solution)/shard_map/pallas_call | solution.py:559
  59.4 3.3 %shard_map.92 = f32[2,2,256,256]{3,2,1,0:T(8,128)} custom-call(s32[1]{0:T(128)S(6)} %copy.10.anum, f32[2048,128]{1,0:T(8,128)} %shard_map.91.tiles), custom_call_target="tpu_custom_call" | custom-call | tf_op jit(solution)/shard_map/pallas_call | solution.py:583

commit v5 on v4

--- a/solution.py
+++ b/solution.py
@@ -22,7 +22,7 @@
 DEPTH = 4
 BLOCK = 4
 UNROLL = 8
-SIDES = [(dx, dy) for dx in (-1, 0, 1) for dy in (-1, 0, 1) if (dx, dy) != (0, 0)]
+SIDES = [(-1, 0), (1, 0), (0, -1), (0, 1), (-1, -1), (-1, 1), (1, -1), (1, 1)]
 
 
 def tables():
@@ -440,7 +440,6 @@
                 sweep(begin_at + steps * UNROLL, rest)
 
     swap(0, 0, "start")
-    swap(0, 1, "start")
     exchange(kap, ksend, krecv, "wait")
 
     row_at = lax.broadcasted_iota(jnp.int32, (40, 128), 0)
@@ -476,6 +475,7 @@
         return carry
 
     lax.fori_loop(1, 23, weights, 0)
+    swap(0, 1, "start")
 
     for p in range(2):
         swap(0, p, "wait")
@@ -535,7 +535,7 @@
 
     def pair(step, carry):
         todo = []
-        for x, xt in [(2 * step + i, xt) for i in range(2) for xt in range(2)]:
+        for x, xt in [(4 * step + i, xt) for i in range(4) for xt in range(2)]:
             row = pl.multiple_of(x * 16 + xt * 8, 8)
             for h in range(2):
                 parts = [
@@ -547,7 +547,7 @@
             out[t, z, pl.ds(row, 8), lane : lane + 128] = value
         return carry
 
-    lax.fori_loop(0, out.shape[2] // 32, pair, 0)
+    lax.fori_loop(0, out.shape[2] // 64, pair, 0)
 
 
 def body(source, start_field, last_guess, classes, conductivity, alpha_num):

time: 62.9 us -> 62 us (0.986)
  Pallas kernels: 62.1 us -> 61.1 us
where the time goes in v5:
time: 62 us; the launch traced here: 61.8 us
  Pallas kernels  61.1 us (99%)
  between operations  0.66 us (1%)
    pallas_call x1, Pallas kernels, body(): pl.pallas_call(kernel, out_shape=jax.ShapeDtypeStruct((2048, 128), F32),...  58.2 us
    pallas_call x1, Pallas kernels, body(): pl.pallas_call(unpack_kernel, grid=(steps,), out_shape=jax.ShapeDtypeStru...  2.96 us

profile of v5, /device:TPU:1, one launch (start us, length us, event | category | flops | bytes accessed | tf_op | source)
XLA Modules:
  0.0 61.8 jit_solution(11901714357916039077)
XLA Ops:
  0.7 58.2 %shard_map.91.tiles = f32[2048,128]{1,0:T(8,128)} custom-call(s32[1]{0:T(128)S(6)} %copy.10.anum, f32[8]{0:T(128)} %cond.1, f32[2,2,256,256]{3,2,1,0:T(8,128)} %source_in.1, f32[2,256,256]{2,1,0:T(8,128)} %start_in.1, f32[2,256,256]{2,1,0:T(8,128)} %guess_in.1, s32[2,256,256]{2,1,0:T(8,128)} %classes_in.1, f32[256,256]{1,0:T(8,128)} %constant.6.clone.dft_in, ...), custom_call_target="tpu_custom_call" | custom-call | tf_op jit(solution)/shard_map/pallas_call | solution.py:559
  58.8 3.0 %shard_map.92 = f32[2,2,256,256]{3,2,1,0:T(8,128)} custom-call(s32[1]{0:T(128)S(6)} %copy.10.anum, f32[2048,128]{1,0:T(8,128)} %shard_map.91.tiles), custom_call_target="tpu_custom_call" | custom-call | tf_op jit(solution)/shard_map/pallas_call | solution.py:583

commit v6 on v5

--- a/solution.py
+++ b/solution.py
@@ -565,8 +565,8 @@
             V((2, 2, 256, 256), F32), V((2, 256, 256), F32), V((2, 256, 256), F32), V((2, 32, 128), jnp.int32),
             V((256, 256), F32), V((256, 256), F32), V((256, 256), BF16), V((256, 256), BF16), V((256, 256), BF16), V((256, 256), BF16), V((16, 128), F32),
             pltpu.SemaphoreType.DMA((7,)),
-            V((2048, 128), F32), V((2048, 128), F32), V((1024, 128), F32), V((1024, 128), F32),
-            V((2, 4, 8, 128), jnp.int32), V((64, 128), jnp.int32),
+            V((2048, 128), F32), V((2064, 128), F32), V((1032, 128), F32), V((1032, 128), F32),
+            V((2, 4, 8, 128), jnp.int32), V((72, 128), jnp.int32),
             V((24, 2, 40, 128), F32), V((24, 2, 40, 128), F32), V((24, 2, 40, 128), F32), V((24, 2, 40, 128), F32),
             V((24, 2, 40, 128), F32),
             V((24, 40, 128), F32), V((24, 40, 128), F32), V((24, 40, 128), F32), V((24, 2, 40, 128), F32),

time: 62 us -> 62 us (level)
  no operation moved by 1% of the time
where the time goes in v6:
time: 62 us; the launch traced here: 61.9 us
  Pallas kernels  61.2 us (99%)
  between operations  0.66 us (1%)
    pallas_call x1, Pallas kernels, body(): pl.pallas_call(kernel, out_shape=jax.ShapeDtypeStruct((2048, 128), F32),...  58.2 us
    pallas_call x1, Pallas kernels, body(): pl.pallas_call(unpack_kernel, grid=(steps,), out_shape=jax.ShapeDtypeStru...  2.96 us

profile of v6, /device:TPU:1, one launch (start us, length us, event | category | flops | bytes accessed | tf_op | source)
XLA Modules:
  0.0 61.9 jit_solution(8817887113027120)
XLA Ops:
  0.7 58.2 %shard_map.91.tiles = f32[2048,128]{1,0:T(8,128)} custom-call(s32[1]{0:T(128)S(6)} %copy.10.anum, f32[8]{0:T(128)} %cond.1, f32[2,2,256,256]{3,2,1,0:T(8,128)} %source_in.1, f32[2,256,256]{2,1,0:T(8,128)} %start_in.1, f32[2,256,256]{2,1,0:T(8,128)} %guess_in.1, s32[2,256,256]{2,1,0:T(8,128)} %classes_in.1, f32[256,256]{1,0:T(8,128)} %constant.6.clone.dft_in, ...), custom_call_target="tpu_custom_call" | custom-call | tf_op jit(solution)/shard_map/pallas_call | solution.py:559
  58.9 3.0 %shard_map.92 = f32[2,2,256,256]{3,2,1,0:T(8,128)} custom-call(s32[1]{0:T(128)S(6)} %copy.10.anum, f32[2048,128]{1,0:T(8,128)} %shard_map.91.tiles), custom_call_target="tpu_custom_call" | custom-call | tf_op jit(solution)/shard_map/pallas_call | solution.py:583
